TPU v7x, 256 devices: a whole 4x4x8 slice. The times are simulated.
256 devices in a mesh: space: 8 (over z), tm: 8 (over y, core), dir: 4 (over x).
Axes of the slice: x: 4, y: 4, z: 8, core: 2. Of those that a mesh axis runs over, the one named last changes fastest.
Arguments:
- right_side: float32 [8, 1024, 2048], P('dir', 'space', 'tm'), may hold values from -6 to 6
- spatial_basis: bfloat16 [1024, 1024], replicated, may hold values from -0.1875 to 0.1875
- temporal_basis: bfloat16 [2048, 2048], replicated, may hold values from -0.125 to 0.125
- spectral_weight: float32 [1024, 2048], P(None, ('space', 'tm')), may hold values from 0.2 to 5
- pierce_nodes: int32 [8, 16, 4, 512], P('dir', 'tm'), may hold values from 0 to 1023
- pierce_weights: float32 [8, 16, 4, 512], P('dir', 'tm'), may hold values from 0.2 to 1
Outputs:
- solution_field: float32 [8, 1024, 2048], P('dir', 'space', 'tm')
- residual: float32 [8, 1024, 2048], P('dir', 'space', 'tm')
All inputs are finite; a program needn't handle non-finite values.
Results may differ from a plain program's by a relative error of at most 0.03.
Values may be sent and summed in bfloat16 or wider, within the bound.
A program may use at most 128 MiB of HBM per device.

v0:
```python
import jax
import jax.numpy as jnp
from jax import lax
from jax.sharding import PartitionSpec as P

TBLK = 128
ITERS = 4


def prior_term(field, spatial_basis, temporal_basis, spectral_weight):
    start_bf = field.astype(jnp.bfloat16)
    regrouped = lax.all_to_all(start_bf, "tm", split_axis=1, concat_axis=2, tiled=True)
    dir_count, row_count, full_time = regrouped.shape
    time_mixed = jnp.dot(
        regrouped.reshape(dir_count * row_count, full_time),
        temporal_basis,
        preferred_element_type=jnp.float32,
    )
    time_mixed = time_mixed.astype(jnp.bfloat16).reshape(dir_count, row_count, full_time)
    all_nodes = lax.all_to_all(time_mixed, ("space", "tm"), split_axis=2, concat_axis=1, tiled=True)
    space_mixed = jnp.einsum(
        "sk,dsl->dkl", spatial_basis, all_nodes, preferred_element_type=jnp.float32
    )
    scaled = (spectral_weight[None] * space_mixed).astype(jnp.bfloat16)
    space_back = jnp.einsum(
        "sk,dkl->dsl", spatial_basis, scaled, preferred_element_type=jnp.float32
    ).astype(jnp.bfloat16)
    node_rows = lax.all_to_all(space_back, ("space", "tm"), split_axis=1, concat_axis=2, tiled=True)
    result = lax.dot_general(
        node_rows.reshape(dir_count * row_count, full_time),
        temporal_basis,
        (((1,), (1,)), ((), ())),
        preferred_element_type=jnp.float32,
    )
    result = result.astype(jnp.bfloat16).reshape(dir_count, row_count, full_time)
    returned = lax.all_to_all(result, "tm", split_axis=2, concat_axis=1, tiled=True)
    return returned.astype(jnp.float32)


def build_incidence(pierce_nodes, pierce_weights, node_ids):
    hits = pierce_nodes[..., None] == node_ids
    return jnp.sum(jnp.where(hits, pierce_weights[..., None], 0.0), axis=2)


def per_device(
    right_side, spatial_basis, temporal_basis, spectral_weight, pierce_nodes, pierce_weights
):
    high = lax.Precision.HIGHEST
    dir_here, nodes_here, slots_here = right_side.shape
    block_count = slots_here // TBLK
    offset = lax.axis_index("space") * nodes_here
    incidence_here = build_incidence(
        pierce_nodes, pierce_weights, offset + jnp.arange(nodes_here, dtype=jnp.int32)
    )
    solution_field = jnp.zeros_like(right_side)
    residual = right_side
    direction = right_side
    res_norm = lax.psum(jnp.sum(residual * residual), ("space", "tm", "dir"))
    for iteration in range(ITERS):
        blocks = direction.reshape(dir_here, nodes_here, block_count, TBLK)
        partial_value = jnp.einsum("dbns,dsbt->dbnt", incidence_here, blocks, precision=high)
        predicted = lax.psum(partial_value.astype(jnp.bfloat16), "space").astype(jnp.float32)
        backed = jnp.einsum("dbns,dbnt->dsbt", incidence_here, predicted, precision=high)
        image = prior_term(
            direction, spatial_basis, temporal_basis, spectral_weight
        ) + backed.reshape(dir_here, nodes_here, slots_here)
        curve = lax.psum(jnp.sum(direction * image), ("space", "tm", "dir"))
        step_size = res_norm / curve
        solution_field = solution_field + step_size * direction
        residual = residual - step_size * image
        new_norm = lax.psum(jnp.sum(residual * residual), ("space", "tm", "dir"))
        direction = residual + new_norm / res_norm * direction
        res_norm = new_norm
    return (solution_field, residual)


def solution(mesh):
    placed = (
        P("dir", "space", "tm"),
        P(),
        P(),
        P(None, ("space", "tm")),
        P("dir", "tm", None, None),
        P("dir", "tm", None, None),
    )
    return jax.shard_map(
        per_device,
        mesh=mesh,
        in_specs=placed,
        out_specs=(P("dir", "space", "tm"), P("dir", "space", "tm")),
        check_vma=False,
    )
```

profile of v0, /device:TPU:4, one launch (start us, length us, event | category | flops | bytes accessed | tf_op | source)
XLA Modules:
  0.0 1163.4 jit_solution(9384244497944406422)
XLA Ops:
  13.6 6.1 all-to-all-done
  19.9 4.9 convolution_convert_fusion.7
  27.3 10.1 all-to-all-start.1
  37.4 4.6 select_reduce_fusion
  42.0 6.4 all-to-all-done.1
  60.6 5.5 all-to-all-start.2
  68.2 8.9 all-to-all-done.2
  83.6 6.7 convolution_convert_fusion.6
  102.1 41.8 %all-reduce.6.cloned.1.call-done = bf16[2,2,512,128]{3,2,1,0:T(8,128)(2,1)} async-done(((bf16[2,2,512,128]{3,2,1,0:T(8,128)(2,1)}), bf16[2,2,512,128]{3,2,1,0:T(8,128)(2,1)}) %all-reduce.6.cloned.1.call-update) | async-done | bytes 524304 | tf_op jit(solution)/shard_map/psum | solution.py:62
  148.2 4.7 reshape.145
  159.8 73.5 %all-reduce = (f32[]{:T(128)}, f32[]{:T(128)}) all-reduce(f32[]{:T(128)} %get-tuple-element.7, f32[]{:T(128)} %get-tuple-element.6), channel_id=1, replica_groups=mesh['space'=8,'tm'=8,'dir'=4] {'space','tm','dir'}, use_global_device_ids=true, to_apply=%region_1.2 | all-reduce | flops 2 | bytes 16 | tf_op jit(solution)/shard_map/psum | solution.py:58
  236.9 73.5 %psum.87 = f32[]{:T(128)} all-reduce(f32[]{:T(128)} %get-tuple-element.20), channel_id=1, replica_groups=mesh['space'=8,'tm'=8,'dir'=4] {'space','tm','dir'}, use_global_device_ids=true, to_apply=%region_7.8 | all-reduce | flops 1 | bytes 8 | tf_op jit(solution)/shard_map/psum | solution.py:71
  313.5 8.8 all_to_all.228
  322.5 5.6 convolution_convert_fusion.5
  335.8 7.0 all-to-all-start.5
  344.6 9.1 all-to-all-done.5
  353.7 4.7 reshape.147
  368.8 5.4 all-to-all-start.6
  377.6 7.7 all-to-all-done.6
  391.7 6.7 convolution_convert_fusion.4
  410.3 42.2 %all-reduce.8.cloned.1.call-done = bf16[2,2,512,128]{3,2,1,0:T(8,128)(2,1)} async-done(((bf16[2,2,512,128]{3,2,1,0:T(8,128)(2,1)}), bf16[2,2,512,128]{3,2,1,0:T(8,128)(2,1)}) %all-reduce.8.cloned.1.call-update) | async-done | bytes 524304 | tf_op jit(solution)/shard_map/psum | solution.py:62
  456.8 4.7 reshape.151
  468.4 73.3 %psum.89 = f32[]{:T(128)} all-reduce(f32[]{:T(128)} %multiply_reduce_fusion.4), channel_id=1, replica_groups=mesh['space'=8,'tm'=8,'dir'=4] {'space','tm','dir'}, use_global_device_ids=true, to_apply=%region_10.11 | all-reduce | flops 1 | bytes 8 | tf_op jit(solution)/shard_map/psum | solution.py:67
  545.4 73.5 %psum.90 = f32[]{:T(128)} all-reduce(f32[]{:T(128)} %get-tuple-element.16), channel_id=1, replica_groups=mesh['space'=8,'tm'=8,'dir'=4] {'space','tm','dir'}, use_global_device_ids=true, to_apply=%region_12.13 | all-reduce | flops 1 | bytes 8 | tf_op jit(solution)/shard_map/psum | solution.py:71
  622.2 8.9 all_to_all.229
  631.2 5.6 convolution_convert_fusion.3
  640.1 4.5 reshape.152
  644.6 7.0 all-to-all-start.9
  653.3 9.1 all-to-all-done.9
  662.5 4.7 reshape.153
  677.6 5.4 all-to-all-start.10
  686.1 7.9 all-to-all-done.10
  700.4 6.7 convolution_convert_fusion.2
  710.4 4.5 reshape.156
  719.0 42.2 %all-reduce.10.cloned.1.call-done = bf16[2,2,512,128]{3,2,1,0:T(8,128)(2,1)} async-done(((bf16[2,2,512,128]{3,2,1,0:T(8,128)(2,1)}), bf16[2,2,512,128]{3,2,1,0:T(8,128)(2,1)}) %all-reduce.10.cloned.1.call-update) | async-done | bytes 524304 | tf_op jit(solution)/shard_map/psum | solution.py:62
  765.5 4.7 reshape.157
  777.0 73.3 %psum.92 = f32[]{:T(128)} all-reduce(f32[]{:T(128)} %multiply_reduce_fusion.2), channel_id=1, replica_groups=mesh['space'=8,'tm'=8,'dir'=4] {'space','tm','dir'}, use_global_device_ids=true, to_apply=%region_15.16 | all-reduce | flops 1 | bytes 8 | tf_op jit(solution)/shard_map/psum | solution.py:67
  853.9 73.7 %psum.93 = f32[]{:T(128)} all-reduce(f32[]{:T(128)} %get-tuple-element.12), channel_id=1, replica_groups=mesh['space'=8,'tm'=8,'dir'=4] {'space','tm','dir'}, use_global_device_ids=true, to_apply=%region_17.18 | all-reduce | flops 1 | bytes 8 | tf_op jit(solution)/shard_map/psum | solution.py:71
  930.8 9.0 all_to_all.230
  939.9 5.6 convolution_convert_fusion.1
  953.3 6.9 all-to-all-start.13
  962.0 9.1 all-to-all-done.13
  971.1 4.7 reshape.159
  986.2 4.6 all-to-all-start.14
  993.8 8.1 all-to-all-done.14
  1006.7 6.6 convolution_convert_fusion
  1024.5 44.6 %all-reduce.12.cloned.1.call-done = bf16[2,2,512,128]{3,2,1,0:T(8,128)(2,1)} async-done(((bf16[2,2,512,128]{3,2,1,0:T(8,128)(2,1)}), bf16[2,2,512,128]{3,2,1,0:T(8,128)(2,1)}) %all-reduce.12.cloned.1.call-update) | async-done | bytes 524304 | tf_op jit(solution)/shard_map/psum | solution.py:62
  1080.1 73.3 %psum.95 = f32[]{:T(128)} all-reduce(f32[]{:T(128)} %multiply_reduce_fusion), channel_id=1, replica_groups=mesh['space'=8,'tm'=8,'dir'=4] {'space','tm','dir'}, use_global_device_ids=true, to_apply=%region_20.21 | all-reduce | flops 1 | bytes 8 | tf_op jit(solution)/shard_map/psum | solution.py:67
  (142 shorter events, 213.6 us)
Async XLA Ops:
  7.2 46.6 %copy-start = (bf16[1024,1024]{1,0:T(8,128)(2,1)S(1)}, bf16[1024,1024]{1,0:T(8,128)(2,1)}, u32[]{:S(2)}) copy-start(bf16[1024,1024]{1,0:T(8,128)(2,1)} %param.7) | copy-start | bytes 6291460
  9.1 10.6 all-to-all-start
  24.8 29.0 %copy-start.10 = (f32[1024,32]{0,1:T(8,128)S(1)}, f32[1024,32]{0,1:T(8,128)}, u32[]{:S(2)}) copy-start(f32[1024,32]{0,1:T(8,128)} %param.9) | copy-start | bytes 393220
  27.3 21.1 %all-to-all-start.1 = ((bf16[64,2,512]{2,1,0:T(2,128)(2,1)}), bf16[64,2,512]{2,1,0:T(2,128)(2,1)S(1)}, u32[]{:S(2)}, u32[]{:S(2)}) async-start(bf16[64,2,512]{2,1,0:T(2,128)(2,1)} %reshape.140), calls=%async_computation.1 | async-start | bytes 262144 | tf_op jit(solution)/shard_map/all_to_all | solution.py:20
  50.2 16.1 %copy-start.1 = (f32[2,128,256]{2,1,0:T(8,128)S(1)}, f32[2,128,256]{2,1,0:T(8,128)}, u32[]{:S(2)}) copy-start(f32[2,128,256]{2,1,0:T(8,128)} %param.6) | copy-start | bytes 786436
  60.6 16.5 %all-to-all-start.2 = ((bf16[64,2,512]{2,1,0:T(2,128)(2,1)}), bf16[64,2,512]{2,1,0:T(2,128)(2,1)}, u32[]{:S(2)}, u32[]{:S(2)}) async-start(bf16[64,2,512]{2,1,0:T(2,128)(2,1)} %reshape.142), calls=%async_computation.2 | async-start | bytes 262144 | tf_op jit(solution)/shard_map/all_to_all | solution.py:28
  66.1 77.8 %all-reduce.6.cloned.1.call-start = ((), (), s32[]{:S(2)}) async-start(), calls=%async_computation.16 | async-start | bytes 1048576 | tf_op jit(solution)/shard_map/psum | solution.py:62
  98.1 50.1 %all-to-all-start.3 = ((bf16[8,2,4096]{2,1,0:T(2,128)(2,1)}), bf16[8,2,4096]{2,1,0:T(2,128)(2,1)}, u32[]{:S(2)}, u32[]{:S(2)}) async-start(bf16[8,2,4096]{2,1,0:T(2,128)(2,1)} %reshape.144), calls=%async_computation.3 | async-start | bytes 262144 | tf_op jit(solution)/shard_map/all_to_all | solution.py:36
  157.3 0.7 copy-start.5
  335.8 17.9 %all-to-all-start.5 = ((bf16[64,2,512]{2,1,0:T(2,128)(2,1)}), bf16[64,2,512]{2,1,0:T(2,128)(2,1)}, u32[]{:S(2)}, u32[]{:S(2)}) async-start(bf16[64,2,512]{2,1,0:T(2,128)(2,1)} %reshape.146), calls=%async_computation.5 | async-start | bytes 262144 | tf_op jit(solution)/shard_map/all_to_all | solution.py:20
  368.8 16.5 %all-to-all-start.6 = ((bf16[64,2,512]{2,1,0:T(2,128)(2,1)}), bf16[64,2,512]{2,1,0:T(2,128)(2,1)}, u32[]{:S(2)}, u32[]{:S(2)}) async-start(bf16[64,2,512]{2,1,0:T(2,128)(2,1)} %reshape.148), calls=%async_computation.6 | async-start | bytes 262144 | tf_op jit(solution)/shard_map/all_to_all | solution.py:28
  374.3 78.3 %all-reduce.8.cloned.1.call-start = ((), (), s32[]{:S(2)}) async-start(), calls=%async_computation.17 | async-start | bytes 1048576 | tf_op jit(solution)/shard_map/psum | solution.py:62
  406.3 50.5 %all-to-all-start.7 = ((bf16[8,2,4096]{2,1,0:T(2,128)(2,1)}), bf16[8,2,4096]{2,1,0:T(2,128)(2,1)}, u32[]{:S(2)}, u32[]{:S(2)}) async-start(bf16[8,2,4096]{2,1,0:T(2,128)(2,1)} %reshape.150), calls=%async_computation.7 | async-start | bytes 262144 | tf_op jit(solution)/shard_map/all_to_all | solution.py:36
  466.0 0.7 copy-start.6
  644.6 17.9 %all-to-all-start.9 = ((bf16[64,2,512]{2,1,0:T(2,128)(2,1)}), bf16[64,2,512]{2,1,0:T(2,128)(2,1)}, u32[]{:S(2)}, u32[]{:S(2)}) async-start(bf16[64,2,512]{2,1,0:T(2,128)(2,1)} %reshape.152), calls=%async_computation.9 | async-start | bytes 262144 | tf_op jit(solution)/shard_map/all_to_all | solution.py:20
  677.6 16.5 %all-to-all-start.10 = ((bf16[64,2,512]{2,1,0:T(2,128)(2,1)}), bf16[64,2,512]{2,1,0:T(2,128)(2,1)}, u32[]{:S(2)}, u32[]{:S(2)}) async-start(bf16[64,2,512]{2,1,0:T(2,128)(2,1)} %reshape.154), calls=%async_computation.10 | async-start | bytes 262144 | tf_op jit(solution)/shard_map/all_to_all | solution.py:28
  683.0 78.2 %all-reduce.10.cloned.1.call-start = ((), (), s32[]{:S(2)}) async-start(), calls=%async_computation.18 | async-start | bytes 1048576 | tf_op jit(solution)/shard_map/psum | solution.py:62
  715.0 50.5 %all-to-all-start.11 = ((bf16[8,2,4096]{2,1,0:T(2,128)(2,1)}), bf16[8,2,4096]{2,1,0:T(2,128)(2,1)}, u32[]{:S(2)}, u32[]{:S(2)}) async-start(bf16[8,2,4096]{2,1,0:T(2,128)(2,1)} %reshape.156), calls=%async_computation.11 | async-start | bytes 262144 | tf_op jit(solution)/shard_map/all_to_all | solution.py:36
  774.6 0.7 copy-start.7
  953.3 17.9 %all-to-all-start.13 = ((bf16[64,2,512]{2,1,0:T(2,128)(2,1)}), bf16[64,2,512]{2,1,0:T(2,128)(2,1)}, u32[]{:S(2)}, u32[]{:S(2)}) async-start(bf16[64,2,512]{2,1,0:T(2,128)(2,1)} %reshape.158), calls=%async_computation.13 | async-start | bytes 262144 | tf_op jit(solution)/shard_map/all_to_all | solution.py:20
  986.2 15.8 %all-to-all-start.14 = ((bf16[64,2,512]{2,1,0:T(2,128)(2,1)}), bf16[64,2,512]{2,1,0:T(2,128)(2,1)S(1)}, u32[]{:S(2)}, u32[]{:S(2)}) async-start(bf16[64,2,512]{2,1,0:T(2,128)(2,1)} %reshape.160), calls=%async_computation.14 | async-start | bytes 262144 | tf_op jit(solution)/shard_map/all_to_all | solution.py:28
  990.8 78.3 %all-reduce.12.cloned.1.call-start = ((), (), s32[]{:S(2)}) async-start(), calls=%async_computation.19 | async-start | bytes 1048576 | tf_op jit(solution)/shard_map/psum | solution.py:62
  1021.1 52.4 %all-to-all-start.15 = ((bf16[8,2,4096]{2,1,0:T(2,128)(2,1)}), bf16[8,2,4096]{2,1,0:T(2,128)(2,1)S(1)}, u32[]{:S(2)}, u32[]{:S(2)}) async-start(bf16[8,2,4096]{2,1,0:T(2,128)(2,1)} %reshape.162), calls=%async_computation.15 | async-start | bytes 262144 | tf_op jit(solution)/shard_map/all_to_all | solution.py:36
  1071.6 6.7 copy-start.4
  1071.6 83.1 %copy-start.2 = (f32[2,128,256]{2,1,0:T(8,128)S(1)}, f32[2,128,256]{2,1,0:T(8,128)}, u32[]{:S(2)}) copy-start(f32[2,128,256]{2,1,0:T(8,128)} %get-tuple-element.19) | copy-start | bytes 786436
  1071.6 83.1 %copy-start.3 = (f32[2,128,256]{2,1,0:T(8,128)S(1)}, f32[2,128,256]{2,1,0:T(8,128)}, u32[]{:S(2)}) copy-start(f32[2,128,256]{2,1,0:T(8,128)} %get-tuple-element.15) | copy-start | bytes 786436
  1071.6 83.1 %copy-start.8 = (f32[2,128,256]{2,1,0:T(8,128)S(1)}, f32[2,128,256]{2,1,0:T(8,128)}, u32[]{:S(2)}) copy-start(f32[2,128,256]{2,1,0:T(8,128)} %get-tuple-element.13) | copy-start | bytes 786436
  1077.7 0.7 copy-start.9
Sparse Core Ops, SparseCore 0:
  69.3 74.6 all-reduce.5
  377.7 74.8 all-reduce.7
  686.2 74.9 all-reduce.9
  994.0 75.1 all-reduce.11
where the time goes:
time: 1180 us; the launch traced here: 1160 us
  blocking collectives  541 us (46%)
  waiting for transfers between devices  244 us (21%)
  local copies, waits for them, and re-layouts  177 us (15%)
  matrix products  80.1 us (7%)
  starting transfers between devices  72.8 us (6%)
  other arithmetic  25.8 us (2%)
  between operations  23.4 us (2%)
    psum x3, blocking collectives, per_device(): new_norm = lax.psum(jnp.sum(residual * residual), ('space', 'tm', 'dir'))  221 us
    psum x3, blocking collectives, per_device(): curve = lax.psum(jnp.sum(direction * image), ('space', 'tm', 'dir'))  220 us
    psum x4, waiting for transfers between devices, per_device(): lax.psum(partial_value.astype(jnp.bfloat16), 'space').astype(jnp.float32)  171 us
    unnamed x55, local copies, waits for them, and re-layouts  88.5 us
    psum x1, blocking collectives, per_device(): res_norm = lax.psum(jnp.sum(residual * residual), ('space', 'tm', 'dir'))  73.5 us
    all_to_all x4, waiting for transfers between devices, prior_term(): lax.all_to_all(time_mixed, ('space', 'tm'), split_axis=2, concat_axis=1,...  33.8 us
    all_to_all x4, waiting for transfers between devices, prior_term(): lax.all_to_all(space_back, ('space', 'tm'), split_axis=1, concat_axis=2,...  32.7 us
    all_to_all x4, starting transfers between devices, prior_term(): lax.all_to_all(time_mixed, ('space', 'tm'), split_axis=2, concat_axis=1,...  30.9 us
  transfers between devices with their start and end apart: 17, of which 13 were waited for; matrix products, arithmetic and copies ran while one was open for 10% of the time, Pallas kernels for 0%

commit v1 on v0

v1 whole, which is shorter than its diff:
```python
import jax
import jax.numpy as jnp
from jax import lax
from jax.experimental import pallas as pl
from jax.experimental.pallas import tpu as pltpu
from jax.sharding import PartitionSpec as P

ITERS = 4
MESH = pl.DeviceIdType.MESH
F32 = jnp.float32
BF16 = jnp.bfloat16
REDUCE_SIZES = (4, 8, 8)


def dot(a, b):
    return jnp.dot(a, b, preferred_element_type=F32)


def swap(a):
    flat = a.reshape(-1, 128)
    return pltpu.roll(flat, 64, 1).reshape(a.shape)


def fold(a):
    return jnp.sum(a.reshape(-1, 8, 128), axis=0)


def total(a):
    return jnp.sum(jnp.sum(a, axis=0, keepdims=True), axis=1, keepdims=True)


def kernel(
    rs_hbm, s_hbm, t_hbm, w_hbm, pn_hbm, pw_hbm,
    xo_ref, ro_ref,
    rs, s4, st, tb, tt4, w_in, pn, pw, pnode, pwgt, g, gt,
    isend, r, x_, d, vb, fsend, frecv, ua, xr, xd, wslot, wf, zb, bsend, brecv, vk,
    pred_r, pred, pb, yacc, red, rr, osend, orecv,
    load_sem, isend_sem, irecv_sem, psend_sem, precv_sem, w1s, w1r, w2s, w2r,
    fs_sem, fr_sem, bs_sem, br_sem, rs_sem, rr_sem, os_sem, or_sem,
):
    z = lax.axis_index("space")
    m = lax.axis_index("tm")
    x = lax.axis_index("dir")
    y, core = m // 2, m % 2
    p = m * 4 + x
    left = lax.broadcasted_iota(jnp.int32, (1, 128), 1) < 64

    def dev(zz, mm, xx):
        return {"space": zz, "tm": mm, "dir": xx}

    def remote(src, dst, ss, rsem, to):
        return pltpu.make_async_remote_copy(
            src_ref=src, dst_ref=dst, send_sem=ss, recv_sem=rsem, device_id=to, device_id_type=MESH
        )

    loads = [
        pltpu.make_async_copy(rs_hbm, rs, load_sem.at[0]),
        pltpu.make_async_copy(pn_hbm, pn, load_sem.at[1]),
        pltpu.make_async_copy(pw_hbm, pw, load_sem.at[2]),
        pltpu.make_async_copy(w_hbm, w_in, load_sem.at[3]),
    ]
    s_loads = [
        pltpu.make_async_copy(s_hbm.at[:, pl.ds(256 * c, 256)], s4.at[c], load_sem.at[4 + c])
        for c in range(4)
    ]
    t_load = pltpu.make_async_copy(t_hbm, tb, load_sem.at[8])
    for copy in loads + s_loads + [t_load]:
        copy.start()

    barrier = pltpu.get_barrier_semaphore()

    def greet(to):
        pl.semaphore_signal(barrier, inc=1, device_id=to, device_id_type=MESH)

    for o in range(1, 32):
        greet(dev(z, (m + o // 4) % 8, (x + o % 4) % 4))
    for o in range(1, 8):
        greet(dev((z + o) % 8, m, x))
    home = z // 2 == x
    for e in range(2):
        for dx in range(4):
            if dx == 0:
                @pl.when(z != 2 * x + e)
                def _():
                    greet(dev(2 * x + e, m, x))
            else:
                greet(dev(2 * x + e, m, (x + dx) % 4))
    for o in range(8):
        if o == 0:
            @pl.when(jnp.logical_not(home))
            def _():
                greet(dev(z, m, z // 2))
        else:
            greet(dev((z + o) % 8, m, z // 2))

    loads[0].wait()
    for e in range(2):
        for h in range(2):
            c = rs[e, :, 128 * h:128 * h + 128]
            top, bottom = c[:64], c[64:]
            isend[4 * e + 2 * h] = jnp.where(left, top, swap(bottom))
            isend[4 * e + 2 * h + 1] = jnp.where(left, swap(top), bottom)
    for copy in loads[1:]:
        copy.wait()

    pl.semaphore_wait(barrier, 54 - 2 * home.astype(jnp.int32))

    for dx in range(4):
        xx = (x + dx) % 4
        for e in range(2):
            slot = 4 * e + xx
            def send():
                remote(isend.at[slot], r.at[z], isend_sem.at[4 * e + dx], irecv_sem,
                       dev(2 * x + e, m, xx)).start()
            if dx == 0:
                pl.when(z != 2 * x + e)(send)

                @pl.when(z == 2 * x + e)
                def _():
                    pltpu.make_async_copy(isend.at[slot], r.at[z], irecv_sem).start()
            else:
                send()
    e_here = z % 2

    @pl.when(home)
    def _():
        for dx in range(1, 4):
            xx = (x + dx) % 4
            remote(pn.at[e_here, xx // 2], pnode, psend_sem.at[dx - 1], precv_sem.at[0], dev(z, m, xx)).start()
            remote(pw.at[e_here, xx // 2], pwgt, psend_sem.at[dx + 2], precv_sem.at[1], dev(z, m, xx)).start()
        pltpu.make_async_copy(pn.at[e_here, x // 2], pnode, precv_sem.at[0]).start()
        pltpu.make_async_copy(pw.at[e_here, x // 2], pwgt, precv_sem.at[1]).start()
    for o in range(1, 8):
        mm = (m + o) % 8
        rows = pl.ds(pl.multiple_of((mm * 4 + x) * 32, 32), 32)
        remote(w_in.at[rows], wslot.at[m], w1s.at[o - 1], w1r, dev(z, mm, x)).start()
    pltpu.make_async_copy(w_in.at[pl.ds(pl.multiple_of(p * 32, 32), 32)], wslot.at[m], w1r).start()

    for c in range(4):
        s_loads[c].wait()
        st[256 * c:256 * c + 256, :] = s4[c].T

    pltpu.make_async_copy(pnode, pnode, precv_sem.at[0]).wait()
    pltpu.make_async_copy(pwgt, pwgt, precv_sem.at[1]).wait()
    nodes, wgts = pnode[...], pwgt[...]
    nodes_t = jnp.concatenate([nodes, nodes], axis=0).astype(F32).T.astype(jnp.int32)
    wgts_t = jnp.concatenate([wgts, wgts], axis=0).T
    for c in range(8):
        ids = lax.broadcasted_iota(jnp.int32, (128, 512), 0) + 128 * c
        acc = jnp.zeros((128, 512), F32)
        for j in range(4):
            acc += jnp.where(nodes[j:j + 1] == ids, wgts[j:j + 1], 0.0)
        gt[128 * c:128 * c + 128, :] = acc.astype(BF16)
        ids = lax.broadcasted_iota(jnp.int32, (512, 128), 1) + 128 * c
        acc = jnp.zeros((512, 128), F32)
        for j in range(4):
            acc += jnp.where(nodes_t[:, j:j + 1] == ids, wgts_t[:, j:j + 1], 0.0)
        g[:, 128 * c:128 * c + 128] = acc.astype(BF16)

    pltpu.make_async_copy(wslot, wslot, w1r).wait()
    own_w = wf.at[z]
    for h in range(2):
        own_w[:, 128 * h:128 * h + 128] = jnp.concatenate([wslot[4 * h + i] for i in range(4)], axis=1)
    for o in range(1, 8):
        remote(wf.at[z], wf.at[z], w2s.at[o - 1], w2r, dev((z + o) % 8, m, x)).start()

    t_load.wait()
    for c in range(4):
        @pl.loop(0, 8)
        def _(i):
            cols = pl.ds(pl.multiple_of(i * 256, 256), 256)
            tt4[c, cols, :] = tb[512 * c:512 * c + 512, cols].T

    x_[...] = jnp.zeros_like(x_)
    d[...] = jnp.zeros_like(d)
    xd[...] = jnp.zeros_like(xd)
    pred[...] = jnp.zeros_like(pred)
    rr[...] = jnp.ones_like(rr)

    pltpu.make_async_copy(r, r, irecv_sem).wait()
    pltpu.make_async_copy(wf.at[pl.ds(0, 7)], wf.at[pl.ds(0, 7)], w2r).wait()

    def reduce_start(kind, step, value):
        n = REDUCE_SIZES[step]
        own = (x, m, z)[step]
        red[kind, step, own] = value
        slot = red.at[kind, step, own]
        for o in range(1, n):
            to = (own + o) % n
            where = (dev(z, m, to), dev(z, to, x), dev(to, m, x))[step]
            remote(slot, slot, rs_sem.at[kind, step], rr_sem.at[kind, step], where).start()

    def reduce_finish(kind, step):
        n = REDUCE_SIZES[step]
        span = red.at[kind, step, pl.ds(0, n - 1)]
        both = remote(span, span, rs_sem.at[kind, step], rr_sem.at[kind, step], dev(z, m, x))
        both.wait_recv()
        both.wait_send()
        return jnp.sum(red[kind, step, 0:n], axis=0)

    def send_row(i, src, dst, ssem, rsem):
        c = (y + i) % 4
        for o in range(8):
            if i == 0 and o == 0:
                continue
            mm = 2 * c + (core + o // 4) % 2
            xx = (x + o % 4) % 4
            remote(src.at[mm * 4 + xx], dst.at[p], ssem, rsem.at[i], dev(z, mm, xx)).start()

    def wait_row(i, buf, rsem):
        span = buf.at[pl.ds(0, 7 if i == 0 else 8)]
        remote(span, span, rsem.at[i], rsem.at[i], dev(z, m, x)).wait_recv()

    def wait_sent(buf, ssem):
        span = buf.at[pl.ds(0, 31)]
        remote(span, span, ssem, ssem, dev(z, m, x)).wait_send()

    @pl.loop(0, ITERS)
    def _(it):
        rv = r[...].reshape(512, 128)
        reduce_start(0, 0, fold(rv * rv))
        rsw = swap(rv)
        vb[:, 0] = jnp.where(left, rv, rsw).astype(BF16).reshape(8, 64, 128)
        vb[:, 1] = jnp.where(left, rsw, rv).astype(BF16).reshape(8, 64, 128)
        vbv = vb[...].reshape(1024, 128)
        for i in range(4):
            c = (y + i) % 4
            u = dot(st[pl.ds(pl.multiple_of(c * 256, 256), 256), :], vbv).reshape(8, 2, 16, 128)
            fsend[pl.ds(c * 8, 8)] = jnp.where(left, u[:, 0], u[:, 1]).astype(BF16)
            send_row(i, fsend, frecv, fs_sem, fr_sem)
        frecv[p] = fsend[p]
        part = reduce_finish(0, 0)
        reduce_start(0, 1, part)
        pred_r[...] = dot(g[...], vbv)
        part = reduce_finish(0, 1)
        reduce_start(0, 2, part)
        for i in range(4):
            c = (y + 4 - i) % 4
            wait_row(i, frecv, fr_sem)
            tiles = frecv[pl.ds(c * 8, 8)].astype(F32)
            swapped = swap(tiles)
            for j in range(4):
                ua[0:16, 128 * j:128 * j + 128] = jnp.where(left, tiles[2 * j], swapped[2 * j + 1]).astype(BF16)
                ua[16:32, 128 * j:128 * j + 128] = jnp.where(left, swapped[2 * j], tiles[2 * j + 1]).astype(BF16)
            xv = dot(ua[...], tb[pl.ds(pl.multiple_of(c * 512, 512), 512), :])
            if i == 0:
                xr[...] = xv
            else:
                xr[...] += xv
        wait_sent(fsend, fs_sem)
        new_norm = total(reduce_finish(0, 2))
        beta = jnp.where(it == 0, 0.0, new_norm / rr[0:1, 0:1])
        rr[...] = jnp.broadcast_to(new_norm, (8, 128))
        pv = pred_r[...] + beta * pred[...]
        pred[...] = pv
        pb[...] = pv.astype(BF16)
        curve = 0.5 * fold(pv * pv)
        for zz in range(8):
            cols = slice(256 * zz, 256 * zz + 256)
            xv = xr[:, cols] + beta * xd[:, cols]
            xd[:, cols] = xv
            wx = wf[zz] * xv
            zb[:, cols] = wx.astype(BF16)
            q = wx * xv
            curve += fold(q[:, :128] + q[:, 128:])
        reduce_start(1, 0, curve)
        zv = zb[...]
        for i in range(4):
            c = (y + i) % 4
            v = dot(zv, tt4[c])
            for j in range(4):
                top, bottom = v[:16, 128 * j:128 * j + 128], v[16:, 128 * j:128 * j + 128]
                bsend[c * 8 + 2 * j] = jnp.where(left, top, swap(bottom)).astype(BF16)
                bsend[c * 8 + 2 * j + 1] = jnp.where(left, swap(top), bottom).astype(BF16)
            send_row(i, bsend, brecv, bs_sem, br_sem)
            if i == 1:
                part = reduce_finish(1, 0)
                reduce_start(1, 1, part)
        brecv[p] = bsend[p]
        part = reduce_finish(1, 1)
        reduce_start(1, 2, part)
        d[...] = r[...] + beta * d[...]
        yacc[...] = dot(gt[...], pb[...])
        for i in range(4):
            c = (y + 4 - i) % 4
            wait_row(i, brecv, br_sem)
            tiles = brecv[pl.ds(c * 8, 8)].astype(F32)
            swapped = swap(tiles)
            vk[:, 0] = jnp.where(left, tiles, swapped).astype(BF16)
            vk[:, 1] = jnp.where(left, swapped, tiles).astype(BF16)
            yacc[...] += dot(s4[c], vk[...].reshape(256, 128))
        wait_sent(bsend, bs_sem)
        alpha = rr[0:1, 0:1] / total(reduce_finish(1, 2))
        ya = yacc[...].reshape(8, 2, 64, 128)
        image = jnp.where(left, ya[:, 0], ya[:, 1])
        x_[...] += alpha * d[...]
        r[...] -= alpha * image

    xv, rv = x_[...], r[...]
    xs, rsw = swap(xv), swap(rv)
    osend[:, 0:64] = jnp.where(left, xv, rsw).astype(BF16)
    osend[:, 64:128] = jnp.where(left, xs, rv).astype(BF16)
    slot_out = (z % 2) * 4 + x
    for o in range(8):
        zz = (z + o) % 8

        def send():
            remote(osend.at[zz], orecv.at[slot_out], os_sem.at[o], or_sem, dev(zz, m, z // 2)).start()
        if o == 0:
            pl.when(jnp.logical_not(home))(send)

            @pl.when(home)
            def _():
                pltpu.make_async_copy(osend.at[zz], orecv.at[slot_out], or_sem).start()
        else:
            send()

    def sent(src, sem):
        remote(src, src, sem, sem, dev(z, m, x)).wait_send()

    for dx in range(4):
        for e in range(2):
            if dx == 0:
                @pl.when(z != 2 * x + e)
                def _():
                    sent(isend.at[0], isend_sem.at[4 * e + dx])
            else:
                sent(isend.at[0], isend_sem.at[4 * e + dx])

    @pl.when(home)
    def _():
        for dx in range(1, 4):
            sent(pn.at[0, 0], psend_sem.at[dx - 1])
            sent(pw.at[0, 0], psend_sem.at[dx + 2])
    for o in range(1, 8):
        sent(w_in.at[pl.ds(0, 32)], w1s.at[o - 1])
        sent(wf.at[0], w2s.at[o - 1])

    pltpu.make_async_copy(orecv, orecv, or_sem).wait()
    for e in range(2):
        for h in range(2):
            a = orecv[4 * e + 2 * h].astype(F32)
            b = orecv[4 * e + 2 * h + 1].astype(F32)
            xo_ref[e, :, 128 * h:128 * h + 128] = jnp.where(left, a, swap(b))
            ro_ref[e, :, 128 * h:128 * h + 128] = jnp.where(left, swap(a), b)
    for o in range(8):
        if o == 0:
            @pl.when(jnp.logical_not(home))
            def _():
                sent(osend.at[0], os_sem.at[o])
        else:
            sent(osend.at[0], os_sem.at[o])


def per_device(right_side, spatial_basis, temporal_basis, spectral_weight, pierce_nodes, pierce_weights):
    vm = pltpu.VMEM
    dma = pltpu.SemaphoreType.DMA
    scratch = [
        vm((2, 128, 256), F32),
        vm((4, 1024, 256), BF16),
        vm((1024, 1024), BF16),
        vm((2048, 2048), BF16),
        vm((4, 2048, 512), BF16),
        vm((1024, 32), F32),
        vm((2, 2, 4, 512), jnp.int32),
        vm((2, 2, 4, 512), F32),
        vm((4, 512), jnp.int32),
        vm((4, 512), F32),
        vm((512, 1024), BF16),
        vm((1024, 512), BF16),
        vm((8, 64, 128), F32),
        vm((8, 64, 128), F32),
        vm((8, 64, 128), F32),
        vm((8, 64, 128), F32),
        vm((8, 2, 64, 128), BF16),
        vm((32, 16, 128), BF16),
        vm((32, 16, 128), BF16),
        vm((32, 512), BF16),
        vm((32, 2048), F32),
        vm((32, 2048), F32),
        vm((8, 32, 32), F32),
        vm((8, 32, 256), F32),
        vm((32, 2048), BF16),
        vm((32, 16, 128), BF16),
        vm((32, 16, 128), BF16),
        vm((8, 2, 16, 128), BF16),
        vm((512, 128), F32),
        vm((512, 128), F32),
        vm((512, 128), BF16),
        vm((1024, 128), F32),
        vm((2, 3, 8, 8, 128), F32),
        vm((8, 128), F32),
        vm((8, 128, 128), BF16),
        vm((8, 128, 128), BF16),
        dma((9,)),
        dma((8,)),
        dma,
        dma((6,)),
        dma((2,)),
        dma((7,)),
        dma,
        dma((7,)),
        dma,
        dma,
        dma((4,)),
        dma,
        dma((4,)),
        dma((2, 3)),
        dma((2, 3)),
        dma((8,)),
        dma,
    ]
    out = jax.ShapeDtypeStruct(right_side.shape, F32)
    return pl.pallas_call(
        kernel,
        out_shape=(out, out),
        in_specs=[pl.BlockSpec(memory_space=pl.ANY)] * 6,
        out_specs=(pl.BlockSpec(memory_space=pltpu.VMEM),) * 2,
        scratch_shapes=scratch,
        name="cg",
        compiler_params=pltpu.CompilerParams(
            collective_id=0, has_side_effects=True, vmem_limit_bytes=56 * 2**20
        ),
    )(right_side, spatial_basis, temporal_basis, spectral_weight, pierce_nodes, pierce_weights)


def solution(mesh):
    placed = (
        P("dir", "space", "tm"),
        P(),
        P(),
        P(None, ("space", "tm")),
        P("dir", "tm", None, None),
        P("dir", "tm", None, None),
    )
    return jax.shard_map(
        per_device,
        mesh=mesh,
        in_specs=placed,
        out_specs=(P("dir", "space", "tm"), P("dir", "space", "tm")),
        check_vma=False,
    )
```

time: 1180 us -> 146 us (0.12); the launches traced: 1160 us -> 145 us
  blocking collectives: 541 us -> 0 us
  waiting for transfers between devices: 244 us -> 0 us
  local copies, waits for them, and re-layouts: 177 us -> 5.23 us
  Pallas kernels: 0 us -> 139 us
  matrix products: 80.1 us -> 0 us
  starting transfers between devices: 72.8 us -> 0 us
  other arithmetic: 25.8 us -> 0 us
  between operations: 23.4 us -> 0.64 us
    psum x7 -> x0, blocking collectives: 514 us -> none  [the longest x3 221 us: per_device(): new_norm = lax.psum(jnp.sum(residual * residual), ('space', 'tm', 'dir'))]
    psum x4 -> x0, waiting for transfers between devices: 171 us -> none  [per_device(): lax.psum(partial_value.astype(jnp.bfloat16), 'space').astype(jnp.float32)]
    pallas_call x0 -> x1, Pallas kernels: none -> 139 us  [per_device(): pl.pallas_call(kernel, out_shape=(out, out), in_specs=[pl.BlockSpec(memor...]
    unnamed x55 -> x3, local copies, waits for them, and re-layouts: 88.5 us -> 5.23 us
    dot_general x20 -> x0, matrix products: 80.1 us -> none  [the longest x4 26.8 us: prior_term(): lax.dot_general(node_rows.reshape(dir_count * row_count, full_time), temp...]
    all_to_all x13 -> x0, waiting for transfers between devices: 72.7 us -> none  [the longest x4 33.8 us: prior_term(): lax.all_to_all(time_mixed, ('space', 'tm'), split_axis=2, concat_axis=1,...]
    all_to_all x13 -> x0, starting transfers between devices: 71.7 us -> none  [the longest x4 30.9 us: prior_term(): lax.all_to_all(time_mixed, ('space', 'tm'), split_axis=2, concat_axis=1,...]
    reshape x16 -> x0, local copies, waits for them, and re-layouts: 39.4 us -> none  [the longest x4 13.1 us: prior_term(): result.astype(jnp.bfloat16).reshape(dir_count, row_count, full_time)]
  transfers between devices with their start and end apart: 17 -> 0, of which waited for: 13 -> 0; matrix products, arithmetic and copies ran while one was open for 10% -> 0% of each run, Pallas kernels for 0% -> 0%
where the time goes in v1:
time: 146 us; the launch traced here: 145 us
  Pallas kernels  139 us (95%)
  local copies, waits for them, and re-layouts  5.23 us (4%)
    pallas_call x1, Pallas kernels, per_device(): pl.pallas_call(kernel, out_shape=(out, out), in_specs=[pl.BlockSpec(memor...  139 us
    unnamed x3, local copies, waits for them, and re-layouts  5.23 us

profile of v1, /device:TPU:4, one launch (start us, length us, event | category | flops | bytes accessed | tf_op | source)
XLA Modules:
  0.0 145.1 jit_solution(1518270040422773875)
XLA Ops:
  0.6 1.9 %copy.8.w_hbm = f32[1024,32]{1,0:T(8,128)} copy(f32[1024,32]{0,1:T(8,128)} %param.9) | data formatting | bytes 262144 | tf_op args[3]
  2.5 139.2 %cg.1 = (f32[2,128,256]{2,1,0:T(8,128)}, f32[2,128,256]{2,1,0:T(8,128)}) custom-call(f32[2,128,256]{2,1,0:T(8,128)} %rs_hbm.1, bf16[1024,1024]{1,0:T(8,128)(2,1)} %s_hbm.1, bf16[2048,2048]{1,0:T(8,128)(2,1)} %t_hbm.1, f32[1024,32]{1,0:T(8,128)} %copy.8.w_hbm, s32[2,2,4,512]{3,2,1,0:T(4,128)} %pn_hbm.1, f32[2,2,4,512]{3,2,1,0:T(4,128)} %pw_hbm.1), custom_call_target="tpu_custom_call" | custom-call | tf_op jit(solution)/shard_map/cg/pallas_call | solution.py:414
  141.8 1.7 %copy.11 = f32[2,128,256]{2,1,0:T(8,128)} copy(f32[2,128,256]{2,1,0:T(8,128)} %get-tuple-element.4) | data formatting | bytes 524288
  143.4 1.7 %copy.12 = f32[2,128,256]{2,1,0:T(8,128)} copy(f32[2,128,256]{2,1,0:T(8,128)} %get-tuple-element.5) | data formatting | bytes 524288

commit v2 on v1

--- a/solution.py
+++ b/solution.py
@@ -9,7 +9,7 @@
 MESH = pl.DeviceIdType.MESH
 F32 = jnp.float32
 BF16 = jnp.bfloat16
-REDUCE_SIZES = (4, 8, 8)
+ROWS = (2, 1, 3, 0)
 
 
 def dot(a, b):
@@ -33,9 +33,9 @@
     rs_hbm, s_hbm, t_hbm, w_hbm, pn_hbm, pw_hbm,
     xo_ref, ro_ref,
     rs, s4, st, tb, tt4, w_in, pn, pw, pnode, pwgt, g, gt,
-    isend, r, x_, d, vb, fsend, frecv, ua, xr, xd, wslot, wf, zb, bsend, brecv, vk,
-    pred_r, pred, pb, yacc, red, rr, osend, orecv,
-    load_sem, isend_sem, irecv_sem, psend_sem, precv_sem, w1s, w1r, w2s, w2r,
+    w_cols, isend, i1, i2, r, x_, d, q, vb, fsend, frecv, ua, xr, xd, wslot, wf, zb, bsend, brecv, vk,
+    pred_r, pred, pb, yacc, red, scal, osend, orecv,
+    load_sem, i1s, i1r, i2s, i2r, psend_sem, precv_sem, w1s, w1r, w2s, w2r,
     fs_sem, fr_sem, bs_sem, br_sem, rs_sem, rr_sem, os_sem, or_sem,
 ):
     z = lax.axis_index("space")
@@ -74,8 +74,8 @@
 
     for o in range(1, 32):
         greet(dev(z, (m + o // 4) % 8, (x + o % 4) % 4))
-    for o in range(1, 8):
-        greet(dev((z + o) % 8, m, x))
+    for o in range(2, 16):
+        greet(dev((z + o // 2) % 8, 2 * y + (core + o) % 2, x))
     home = z // 2 == x
     for e in range(2):
         for dx in range(4):
@@ -94,32 +94,21 @@
             greet(dev((z + o) % 8, m, z // 2))
 
     loads[0].wait()
-    for e in range(2):
-        for h in range(2):
+    for h in range(2):
+        for e in range(2):
             c = rs[e, :, 128 * h:128 * h + 128]
             top, bottom = c[:64], c[64:]
-            isend[4 * e + 2 * h] = jnp.where(left, top, swap(bottom))
-            isend[4 * e + 2 * h + 1] = jnp.where(left, swap(top), bottom)
+            isend[2 * h, e] = jnp.where(left, top, swap(bottom)).astype(BF16)
+            isend[2 * h + 1, e] = jnp.where(left, swap(top), bottom).astype(BF16)
+    i1[pl.ds(2 * x, 2)] = isend[x]
     for copy in loads[1:]:
         copy.wait()
 
-    pl.semaphore_wait(barrier, 54 - 2 * home.astype(jnp.int32))
-
-    for dx in range(4):
+    pl.semaphore_wait(barrier, 61 - 2 * home.astype(jnp.int32))
+
+    for dx in (2, 1, 3):
         xx = (x + dx) % 4
-        for e in range(2):
-            slot = 4 * e + xx
-            def send():
-                remote(isend.at[slot], r.at[z], isend_sem.at[4 * e + dx], irecv_sem,
-                       dev(2 * x + e, m, xx)).start()
-            if dx == 0:
-                pl.when(z != 2 * x + e)(send)
-
-                @pl.when(z == 2 * x + e)
-                def _():
-                    pltpu.make_async_copy(isend.at[slot], r.at[z], irecv_sem).start()
-            else:
-                send()
+        remote(isend.at[xx], i1.at[pl.ds(2 * x, 2)], i1s.at[dx - 1], i1r.at[dx - 1], dev(z, m, xx)).start()
     e_here = z % 2
 
     @pl.when(home)
@@ -130,15 +119,33 @@
             remote(pw.at[e_here, xx // 2], pwgt, psend_sem.at[dx + 2], precv_sem.at[1], dev(z, m, xx)).start()
         pltpu.make_async_copy(pn.at[e_here, x // 2], pnode, precv_sem.at[0]).start()
         pltpu.make_async_copy(pw.at[e_here, x // 2], pwgt, precv_sem.at[1]).start()
+    w_cols[...] = w_in[...].T.reshape(32, 32, 32)
     for o in range(1, 8):
         mm = (m + o) % 8
-        rows = pl.ds(pl.multiple_of((mm * 4 + x) * 32, 32), 32)
-        remote(w_in.at[rows], wslot.at[m], w1s.at[o - 1], w1r, dev(z, mm, x)).start()
-    pltpu.make_async_copy(w_in.at[pl.ds(pl.multiple_of(p * 32, 32), 32)], wslot.at[m], w1r).start()
-
+        remote(w_cols.at[mm * 4 + x], wslot.at[m], w1s.at[o - 1], w1r, dev(z, mm, x)).start()
+    pltpu.make_async_copy(w_cols.at[p], wslot.at[m], w1r).start()
+
+    def forward(xx):
+        for e in range(2):
+            zz = 2 * xx + e
+
+            @pl.when(zz != z)
+            def _():
+                remote(i1.at[zz], i2.at[z], i2s.at[(zz + 7 - z) % 8], i2r, dev(zz, m, x)).start()
+
+            @pl.when(zz == z)
+            def _():
+                pltpu.make_async_copy(i1.at[zz], i2.at[z], i2r).start()
+
+    forward(x)
     for c in range(4):
         s_loads[c].wait()
         st[256 * c:256 * c + 256, :] = s4[c].T
+    for dx in (1, 3, 2):
+        xx = (x + 4 - dx) % 4
+        span = i1.at[pl.ds(2 * xx, 2)]
+        remote(span, span, i1s.at[dx - 1], i1r.at[dx - 1], dev(z, m, x)).wait_recv()
+        forward(xx)
 
     pltpu.make_async_copy(pnode, pnode, precv_sem.at[0]).wait()
     pltpu.make_async_copy(pwgt, pwgt, precv_sem.at[1]).wait()
@@ -171,45 +178,43 @@
             cols = pl.ds(pl.multiple_of(i * 256, 256), 256)
             tt4[c, cols, :] = tb[512 * c:512 * c + 512, cols].T
 
-    x_[...] = jnp.zeros_like(x_)
-    d[...] = jnp.zeros_like(d)
-    xd[...] = jnp.zeros_like(xd)
-    pred[...] = jnp.zeros_like(pred)
-    rr[...] = jnp.ones_like(rr)
-
-    pltpu.make_async_copy(r, r, irecv_sem).wait()
-    pltpu.make_async_copy(wf.at[pl.ds(0, 7)], wf.at[pl.ds(0, 7)], w2r).wait()
-
-    def reduce_start(kind, step, value):
-        n = REDUCE_SIZES[step]
-        own = (x, m, z)[step]
-        red[kind, step, own] = value
-        slot = red.at[kind, step, own]
-        for o in range(1, n):
-            to = (own + o) % n
-            where = (dev(z, m, to), dev(z, to, x), dev(to, m, x))[step]
-            remote(slot, slot, rs_sem.at[kind, step], rr_sem.at[kind, step], where).start()
-
-    def reduce_finish(kind, step):
-        n = REDUCE_SIZES[step]
-        span = red.at[kind, step, pl.ds(0, n - 1)]
-        both = remote(span, span, rs_sem.at[kind, step], rr_sem.at[kind, step], dev(z, m, x))
+    for ref in (x_, d, q, xr, xd, pred_r, pred):
+        ref[...] = jnp.zeros_like(ref)
+    scal[...] = jnp.ones_like(scal)
+
+    pltpu.make_async_copy(i2, i2, i2r).wait()
+    r[...] = i2[...].astype(F32)
+
+    def reduce_start(par, step, value):
+        own = (y * 4 + x, z * 2 + core)[step]
+        slot = red.at[par, step, own]
+        slot[...] = value
+        for o in range(1, 16):
+            if step == 0:
+                where = dev(z, 2 * ((y + o // 4) % 4) + core, (x + o % 4) % 4)
+            else:
+                where = dev((z + o // 2) % 8, 2 * y + (core + o) % 2, x)
+            remote(slot, slot, rs_sem.at[par, step], rr_sem.at[par, step], where).start()
+
+    def reduce_finish(par, step):
+        span = red.at[par, step, pl.ds(0, 15)]
+        both = remote(span, span, rs_sem.at[par, step], rr_sem.at[par, step], dev(z, m, x))
         both.wait_recv()
         both.wait_send()
-        return jnp.sum(red[kind, step, 0:n], axis=0)
-
-    def send_row(i, src, dst, ssem, rsem):
-        c = (y + i) % 4
+        return jnp.sum(red[par, step], axis=0)
+
+    def send_row(dy, src, dst, ssem, rsem):
+        c = (y + dy) % 4
         for o in range(8):
-            if i == 0 and o == 0:
+            if dy == 0 and o == 0:
                 continue
             mm = 2 * c + (core + o // 4) % 2
             xx = (x + o % 4) % 4
-            remote(src.at[mm * 4 + xx], dst.at[p], ssem, rsem.at[i], dev(z, mm, xx)).start()
-
-    def wait_row(i, buf, rsem):
-        span = buf.at[pl.ds(0, 7 if i == 0 else 8)]
-        remote(span, span, rsem.at[i], rsem.at[i], dev(z, m, x)).wait_recv()
+            remote(src.at[mm * 4 + xx], dst.at[p], ssem, rsem.at[dy], dev(z, mm, xx)).start()
+
+    def wait_row(dy, buf, rsem):
+        span = buf.at[pl.ds(0, 7 if dy == 0 else 8)]
+        remote(span, span, rsem.at[dy], rsem.at[dy], dev(z, m, x)).wait_recv()
 
     def wait_sent(buf, ssem):
         span = buf.at[pl.ds(0, 31)]
@@ -217,84 +222,96 @@
 
     @pl.loop(0, ITERS)
     def _(it):
+        par = it % 2
         rv = r[...].reshape(512, 128)
-        reduce_start(0, 0, fold(rv * rv))
         rsw = swap(rv)
         vb[:, 0] = jnp.where(left, rv, rsw).astype(BF16).reshape(8, 64, 128)
         vb[:, 1] = jnp.where(left, rsw, rv).astype(BF16).reshape(8, 64, 128)
         vbv = vb[...].reshape(1024, 128)
-        for i in range(4):
-            c = (y + i) % 4
+        for dy in ROWS:
+            c = (y + dy) % 4
             u = dot(st[pl.ds(pl.multiple_of(c * 256, 256), 256), :], vbv).reshape(8, 2, 16, 128)
             fsend[pl.ds(c * 8, 8)] = jnp.where(left, u[:, 0], u[:, 1]).astype(BF16)
-            send_row(i, fsend, frecv, fs_sem, fr_sem)
+            send_row(dy, fsend, frecv, fs_sem, fr_sem)
         frecv[p] = fsend[p]
-        part = reduce_finish(0, 0)
-        reduce_start(0, 1, part)
-        pred_r[...] = dot(g[...], vbv)
-        part = reduce_finish(0, 1)
-        reduce_start(0, 2, part)
-        for i in range(4):
-            c = (y + 4 - i) % 4
-            wait_row(i, frecv, fr_sem)
+        beta = scal[2, 0:1, 0:1]
+        xd[...] = xr[...] + beta * xd[...]
+        pold = pred_r[...] + beta * pred[...]
+        pred[...] = pold
+        pnew = dot(g[...], vbv)
+        pred_r[...] = pnew
+        pb[...] = pnew.astype(BF16)
+        norm = fold(rv * rv)
+        suma = 0.5 * fold(pnew * pnew)
+        sumb = 0.5 * fold(pnew * pold)
+        for n, dy in enumerate(ROWS):
+            c = (y + 4 - dy) % 4
+            wait_row(dy, frecv, fr_sem)
             tiles = frecv[pl.ds(c * 8, 8)].astype(F32)
             swapped = swap(tiles)
             for j in range(4):
                 ua[0:16, 128 * j:128 * j + 128] = jnp.where(left, tiles[2 * j], swapped[2 * j + 1]).astype(BF16)
                 ua[16:32, 128 * j:128 * j + 128] = jnp.where(left, swapped[2 * j], tiles[2 * j + 1]).astype(BF16)
             xv = dot(ua[...], tb[pl.ds(pl.multiple_of(c * 512, 512), 512), :])
-            if i == 0:
+            if n == 0:
                 xr[...] = xv
             else:
                 xr[...] += xv
         wait_sent(fsend, fs_sem)
-        new_norm = total(reduce_finish(0, 2))
-        beta = jnp.where(it == 0, 0.0, new_norm / rr[0:1, 0:1])
-        rr[...] = jnp.broadcast_to(new_norm, (8, 128))
-        pv = pred_r[...] + beta * pred[...]
-        pred[...] = pv
-        pb[...] = pv.astype(BF16)
-        curve = 0.5 * fold(pv * pv)
+
+        @pl.when(it == 0)
+        def _():
+            pltpu.make_async_copy(wf.at[pl.ds(0, 7)], wf.at[pl.ds(0, 7)], w2r).wait()
+
         for zz in range(8):
             cols = slice(256 * zz, 256 * zz + 256)
-            xv = xr[:, cols] + beta * xd[:, cols]
-            xd[:, cols] = xv
+            xv = xr[:, cols]
             wx = wf[zz] * xv
             zb[:, cols] = wx.astype(BF16)
-            q = wx * xv
-            curve += fold(q[:, :128] + q[:, 128:])
-        reduce_start(1, 0, curve)
+            qa, qb = wx * xv, wx * xd[:, cols]
+            suma += fold(qa[:, :128] + qa[:, 128:])
+            sumb += fold(qb[:, :128] + qb[:, 128:])
+        row = lax.broadcasted_iota(jnp.int32, (8, 128), 0)
+        one = [jnp.sum(part, axis=0, keepdims=True) for part in (norm, suma, sumb)]
+        reduce_start(par, 0, jnp.where(row == 0, one[0], jnp.where(row == 1, one[1], one[2])))
         zv = zb[...]
-        for i in range(4):
-            c = (y + i) % 4
+        for n, dy in enumerate(ROWS):
+            c = (y + dy) % 4
             v = dot(zv, tt4[c])
             for j in range(4):
                 top, bottom = v[:16, 128 * j:128 * j + 128], v[16:, 128 * j:128 * j + 128]
                 bsend[c * 8 + 2 * j] = jnp.where(left, top, swap(bottom)).astype(BF16)
                 bsend[c * 8 + 2 * j + 1] = jnp.where(left, swap(top), bottom).astype(BF16)
-            send_row(i, bsend, brecv, bs_sem, br_sem)
-            if i == 1:
-                part = reduce_finish(1, 0)
-                reduce_start(1, 1, part)
+            send_row(dy, bsend, brecv, bs_sem, br_sem)
+            if n == 2:
+                part = reduce_finish(par, 0)
+                reduce_start(par, 1, part)
         brecv[p] = bsend[p]
-        part = reduce_finish(1, 1)
-        reduce_start(1, 2, part)
-        d[...] = r[...] + beta * d[...]
         yacc[...] = dot(gt[...], pb[...])
-        for i in range(4):
-            c = (y + 4 - i) % 4
-            wait_row(i, brecv, br_sem)
+        for dy in ROWS:
+            c = (y + 4 - dy) % 4
+            wait_row(dy, brecv, br_sem)
             tiles = brecv[pl.ds(c * 8, 8)].astype(F32)
             swapped = swap(tiles)
             vk[:, 0] = jnp.where(left, tiles, swapped).astype(BF16)
             vk[:, 1] = jnp.where(left, swapped, tiles).astype(BF16)
             yacc[...] += dot(s4[c], vk[...].reshape(256, 128))
         wait_sent(bsend, bs_sem)
-        alpha = rr[0:1, 0:1] / total(reduce_finish(1, 2))
+        sums = jnp.sum(reduce_finish(par, 1), axis=1, keepdims=True)
+        rr, ra, rb = sums[0:1], sums[1:2], sums[2:3]
+        beta = jnp.where(it == 0, 0.0, rr / scal[0, 0:1, 0:1])
+        curve = ra + beta * (2.0 * rb + beta * scal[1, 0:1, 0:1])
+        alpha = rr / curve
+        scal[0] = jnp.broadcast_to(rr, (8, 128))
+        scal[1] = jnp.broadcast_to(curve, (8, 128))
+        scal[2] = jnp.broadcast_to(beta, (8, 128))
         ya = yacc[...].reshape(8, 2, 64, 128)
-        image = jnp.where(left, ya[:, 0], ya[:, 1])
-        x_[...] += alpha * d[...]
-        r[...] -= alpha * image
+        qv = jnp.where(left, ya[:, 0], ya[:, 1]) + beta * q[...]
+        q[...] = qv
+        dv = r[...] + beta * d[...]
+        d[...] = dv
+        x_[...] += alpha * dv
+        r[...] -= alpha * qv
 
     xv, rv = x_[...], r[...]
     xs, rsw = swap(xv), swap(rv)
@@ -318,14 +335,10 @@
     def sent(src, sem):
         remote(src, src, sem, sem, dev(z, m, x)).wait_send()
 
-    for dx in range(4):
-        for e in range(2):
-            if dx == 0:
-                @pl.when(z != 2 * x + e)
-                def _():
-                    sent(isend.at[0], isend_sem.at[4 * e + dx])
-            else:
-                sent(isend.at[0], isend_sem.at[4 * e + dx])
+    for o in range(3):
+        sent(isend.at[0], i1s.at[o])
+    for o in range(7):
+        sent(i1.at[0], i2s.at[o])
 
     @pl.when(home)
     def _():
@@ -333,7 +346,7 @@
             sent(pn.at[0, 0], psend_sem.at[dx - 1])
             sent(pw.at[0, 0], psend_sem.at[dx + 2])
     for o in range(1, 8):
-        sent(w_in.at[pl.ds(0, 32)], w1s.at[o - 1])
+        sent(w_cols.at[0], w1s.at[o - 1])
         sent(wf.at[0], w2s.at[o - 1])
 
     pltpu.make_async_copy(orecv, orecv, or_sem).wait()
@@ -361,13 +374,17 @@
         vm((1024, 1024), BF16),
         vm((2048, 2048), BF16),
         vm((4, 2048, 512), BF16),
-        vm((1024, 32), F32),
+        vm((32, 1024), F32),
         vm((2, 2, 4, 512), jnp.int32),
         vm((2, 2, 4, 512), F32),
         vm((4, 512), jnp.int32),
         vm((4, 512), F32),
         vm((512, 1024), BF16),
         vm((1024, 512), BF16),
+        vm((32, 32, 32), F32),
+        vm((4, 2, 64, 128), BF16),
+        vm((8, 64, 128), BF16),
+        vm((8, 64, 128), BF16),
         vm((8, 64, 128), F32),
         vm((8, 64, 128), F32),
         vm((8, 64, 128), F32),
@@ -388,12 +405,14 @@
         vm((512, 128), F32),
         vm((512, 128), BF16),
         vm((1024, 128), F32),
-        vm((2, 3, 8, 8, 128), F32),
-        vm((8, 128), F32),
+        vm((2, 2, 16, 8, 128), F32),
+        vm((3, 8, 128), F32),
         vm((8, 128, 128), BF16),
         vm((8, 128, 128), BF16),
         dma((9,)),
-        dma((8,)),
+        dma((3,)),
+        dma((3,)),
+        dma((7,)),
         dma,
         dma((6,)),
         dma((2,)),
@@ -405,8 +424,8 @@
         dma((4,)),
         dma,
         dma((4,)),
-        dma((2, 3)),
-        dma((2, 3)),
+        dma((2, 2)),
+        dma((2, 2)),
         dma((8,)),
         dma,
     ]
@@ -421,7 +440,7 @@
         compiler_params=pltpu.CompilerParams(
             collective_id=0, has_side_effects=True, vmem_limit_bytes=56 * 2**20
         ),
-    )(right_side, spatial_basis, temporal_basis, spectral_weight, pierce_nodes, pierce_weights)
+    )(right_side, spatial_basis, temporal_basis, spectral_weight.T, pierce_nodes, pierce_weights)
 
 
 def solution(mesh):

time: 146 us -> 108 us (0.74)
  Pallas kernels: 139 us -> 103 us
  local copies, waits for them, and re-layouts: 5.23 us -> 3.34 us
    pallas_call x1, Pallas kernels: 139 us -> 103 us  [per_device(): pl.pallas_call(kernel, out_shape=(out, out), in_specs=[pl.BlockSpec(memor...]
    unnamed x3 -> x2, local copies, waits for them, and re-layouts: 5.23 us -> 3.34 us
where the time goes in v2:
time: 108 us; the launch traced here: 107 us
  Pallas kernels  103 us (95%)
  local copies, waits for them, and re-layouts  3.34 us (3%)
    pallas_call x1, Pallas kernels, per_device(): pl.pallas_call(kernel, out_shape=(out, out), in_specs=[pl.BlockSpec(memor...  103 us
    unnamed x2, local copies, waits for them, and re-layouts  3.34 us

profile of v2, /device:TPU:4, one launch (start us, length us, event | category | flops | bytes accessed | tf_op | source)
XLA Modules:
  0.0 107.4 jit_solution(2178464066922674216)
XLA Ops:
  0.6 103.4 %cg.1 = (f32[2,128,256]{2,1,0:T(8,128)}, f32[2,128,256]{2,1,0:T(8,128)}) custom-call(f32[2,128,256]{2,1,0:T(8,128)} %rs_hbm.1, bf16[1024,1024]{1,0:T(8,128)(2,1)} %s_hbm.1, bf16[2048,2048]{1,0:T(8,128)(2,1)} %t_hbm.1, f32[32,1024]{1,0:T(8,128)} %bitcast.1, s32[2,2,4,512]{3,2,1,0:T(4,128)} %pn_hbm.1, f32[2,2,4,512]{3,2,1,0:T(4,128)} %pw_hbm.1), custom_call_target="tpu_custom_call" | custom-call | tf_op jit(solution)/shard_map/cg/pallas_call | solution.py:433
  104.0 1.7 %copy.10 = f32[2,128,256]{2,1,0:T(8,128)} copy(f32[2,128,256]{2,1,0:T(8,128)} %get-tuple-element.4) | data formatting | bytes 524288
  105.7 1.7 %copy.11 = f32[2,128,256]{2,1,0:T(8,128)} copy(f32[2,128,256]{2,1,0:T(8,128)} %get-tuple-element.5) | data formatting | bytes 524288

commit v3 on v2

--- a/solution.py
+++ b/solution.py
@@ -33,8 +33,8 @@
     rs_hbm, s_hbm, t_hbm, w_hbm, pn_hbm, pw_hbm,
     xo_ref, ro_ref,
     rs, s4, st, tb, tt4, w_in, pn, pw, pnode, pwgt, g, gt,
-    w_cols, isend, i1, i2, r, x_, d, q, vb, fsend, frecv, ua, xr, xd, wslot, wf, zb, bsend, brecv, vk,
-    pred_r, pred, pb, yacc, red, scal, osend, orecv,
+    w_cols, isend, i1, i2, im, r, q, vb, fsend, frecv, ua, xv_, xm, xq, xd, wslot, wf, zb, bsend, brecv, vk,
+    pr, pq, pd, pb, yacc, red, scal, xb, db, qb, osend, orecv, olast,
     load_sem, i1s, i1r, i2s, i2r, psend_sem, precv_sem, w1s, w1r, w2s, w2r,
     fs_sem, fr_sem, bs_sem, br_sem, rs_sem, rr_sem, os_sem, or_sem,
 ):
@@ -103,6 +103,7 @@
     i1[pl.ds(2 * x, 2)] = isend[x]
     for copy in loads[1:]:
         copy.wait()
+    w_cols[...] = w_in[...].T.reshape(32, 32, 32)
 
     pl.semaphore_wait(barrier, 61 - 2 * home.astype(jnp.int32))
 
@@ -119,7 +120,6 @@
             remote(pw.at[e_here, xx // 2], pwgt, psend_sem.at[dx + 2], precv_sem.at[1], dev(z, m, xx)).start()
         pltpu.make_async_copy(pn.at[e_here, x // 2], pnode, precv_sem.at[0]).start()
         pltpu.make_async_copy(pw.at[e_here, x // 2], pwgt, precv_sem.at[1]).start()
-    w_cols[...] = w_in[...].T.reshape(32, 32, 32)
     for o in range(1, 8):
         mm = (m + o) % 8
         remote(w_cols.at[mm * 4 + x], wslot.at[m], w1s.at[o - 1], w1r, dev(z, mm, x)).start()
@@ -146,6 +146,19 @@
         span = i1.at[pl.ds(2 * xx, 2)]
         remote(span, span, i1s.at[dx - 1], i1r.at[dx - 1], dev(z, m, x)).wait_recv()
         forward(xx)
+
+    pltpu.make_async_copy(wslot, wslot, w1r).wait()
+    own_w = wf.at[z]
+    for h in range(2):
+        own_w[:, 128 * h:128 * h + 128] = jnp.concatenate([wslot[4 * h + i] for i in range(4)], axis=1)
+    for o in range(1, 8):
+        remote(wf.at[z], wf.at[z], w2s.at[o - 1], w2r, dev((z + o) % 8, m, x)).start()
+
+    for ref in (r, q, xm, xq, xd, pr, pq, pd, xb, db, qb):
+        ref[...] = jnp.zeros_like(ref)
+    scal[0:2] = jnp.ones((2, 8, 128), F32)
+    scal[2] = jnp.full((8, 128), -1.0, F32)
+    scal[3] = jnp.zeros((8, 128), F32)
 
     pltpu.make_async_copy(pnode, pnode, precv_sem.at[0]).wait()
     pltpu.make_async_copy(pwgt, pwgt, precv_sem.at[1]).wait()
@@ -164,26 +177,18 @@
             acc += jnp.where(nodes_t[:, j:j + 1] == ids, wgts_t[:, j:j + 1], 0.0)
         g[:, 128 * c:128 * c + 128] = acc.astype(BF16)
 
-    pltpu.make_async_copy(wslot, wslot, w1r).wait()
-    own_w = wf.at[z]
-    for h in range(2):
-        own_w[:, 128 * h:128 * h + 128] = jnp.concatenate([wslot[4 * h + i] for i in range(4)], axis=1)
-    for o in range(1, 8):
-        remote(wf.at[z], wf.at[z], w2s.at[o - 1], w2r, dev((z + o) % 8, m, x)).start()
-
-    t_load.wait()
-    for c in range(4):
+    def transpose(c):
         @pl.loop(0, 8)
         def _(i):
             cols = pl.ds(pl.multiple_of(i * 256, 256), 256)
             tt4[c, cols, :] = tb[512 * c:512 * c + 512, cols].T
 
-    for ref in (x_, d, q, xr, xd, pred_r, pred):
-        ref[...] = jnp.zeros_like(ref)
-    scal[...] = jnp.ones_like(scal)
+    t_load.wait()
+    for c in range(2):
+        transpose(c)
 
     pltpu.make_async_copy(i2, i2, i2r).wait()
-    r[...] = i2[...].astype(F32)
+    im[...] = i2[...].astype(F32)
 
     def reduce_start(par, step, value):
         own = (y * 4 + x, z * 2 + core)[step]
@@ -220,13 +225,68 @@
         span = buf.at[pl.ds(0, 31)]
         remote(span, span, ssem, ssem, dev(z, m, x)).wait_send()
 
+    def scalars(j):
+        sums = jnp.sum(reduce_finish(j % 2, 1), axis=1, keepdims=True)
+        rr, ra, rb = sums[0:1], sums[1:2], sums[2:3]
+        beta = jnp.where(j == 0, 0.0, rr / scal[0, 0:1, 0:1])
+        curve = ra + beta * (2.0 * rb + beta * scal[1, 0:1, 0:1])
+        for n, value in enumerate((rr, curve, rr / curve, beta)):
+            scal[n] = jnp.broadcast_to(value, (8, 128))
+
+    def factors():
+        return scal[2, 0:1, 0:1], scal[3, 0:1, 0:1]
+
+    slot_out = (z % 2) * 4 + x
+
+    def ship(src, dst, sem):
+        for o in range(8):
+            zz = (z + o) % 8
+
+            def send():
+                remote(src.at[zz], dst.at[slot_out], os_sem.at[o], sem, dev(zz, m, z // 2)).start()
+            if o == 0:
+                pl.when(jnp.logical_not(home))(send)
+
+                @pl.when(home)
+                def _():
+                    pltpu.make_async_copy(src.at[zz], dst.at[slot_out], sem).start()
+            else:
+                send()
+
+    def shipped(src, dst, sem):
+        pltpu.make_async_copy(dst, dst, sem).wait()
+        for o in range(8):
+            if o == 0:
+                @pl.when(jnp.logical_not(home))
+                def _():
+                    sent(src.at[0], os_sem.at[o])
+            else:
+                sent(src.at[0], os_sem.at[o])
+
+    def sent(src, sem):
+        remote(src, src, sem, sem, dev(z, m, x)).wait_send()
+
+    def advance(tiles, x_out, r_out):
+        alpha, beta = factors()
+        for e in range(2):
+            for h in range(2):
+                a, b = tiles[4 * e + 2 * h].astype(F32), tiles[4 * e + 2 * h + 1].astype(F32)
+                for part, rows in ((jnp.where(left, a, swap(b)), slice(0, 64)), (jnp.where(left, swap(a), b), slice(64, 128))):
+                    at = (e, rows, slice(128 * h, 128 * h + 128))
+                    qn = part + beta * qb[at]
+                    dn = rs[at] + beta * db[at]
+                    qb[at] = qn
+                    db[at] = dn
+                    x_out[at] = xb[at] + alpha * dn
+                    r_out[at] = rs[at] - alpha * qn
+
     @pl.loop(0, ITERS)
     def _(it):
         par = it % 2
-        rv = r[...].reshape(512, 128)
-        rsw = swap(rv)
-        vb[:, 0] = jnp.where(left, rv, rsw).astype(BF16).reshape(8, 64, 128)
-        vb[:, 1] = jnp.where(left, rsw, rv).astype(BF16).reshape(8, 64, 128)
+        v = im[...].reshape(512, 128)
+        vsw = swap(v)
+        vb[:, 0] = jnp.where(left, v, vsw).astype(BF16).reshape(8, 64, 128)
+        vb[:, 1] = jnp.where(left, vsw, v).astype(BF16).reshape(8, 64, 128)
         vbv = vb[...].reshape(1024, 128)
         for dy in ROWS:
             c = (y + dy) % 4
@@ -234,16 +294,38 @@
             fsend[pl.ds(c * 8, 8)] = jnp.where(left, u[:, 0], u[:, 1]).astype(BF16)
             send_row(dy, fsend, frecv, fs_sem, fr_sem)
         frecv[p] = fsend[p]
-        beta = scal[2, 0:1, 0:1]
-        xd[...] = xr[...] + beta * xd[...]
-        pold = pred_r[...] + beta * pred[...]
-        pred[...] = pold
-        pnew = dot(g[...], vbv)
-        pred_r[...] = pnew
+
+        @pl.when(it == 0)
+        def _():
+            for c in range(2, 4):
+                transpose(c)
+
+        @pl.when(it > 0)
+        def _():
+            ship(im, orecv.at[it - 1], or_sem.at[it - 1])
+
+        pv = dot(g[...], vbv)
+
+        @pl.when(it > 0)
+        def _():
+            scalars(it - 1)
+
+        alpha, beta = factors()
+        pold = pr[...] + beta * pd[...]
+        pd[...] = pold
+        pqn = pv + beta * pq[...]
+        pq[...] = pqn
+        pnew = pr[...] - alpha * pqn
+        pr[...] = pnew
         pb[...] = pnew.astype(BF16)
-        norm = fold(rv * rv)
+        qn = v + beta * q[...].reshape(512, 128)
+        q[...] = qn.reshape(8, 64, 128)
+        rn = r[...].reshape(512, 128) - alpha * qn
+        r[...] = rn.reshape(8, 64, 128)
+        norm = fold(rn * rn)
         suma = 0.5 * fold(pnew * pnew)
         sumb = 0.5 * fold(pnew * pold)
+        xd[...] = xm[...] + beta * xd[...]
         for n, dy in enumerate(ROWS):
             c = (y + 4 - dy) % 4
             wait_row(dy, frecv, fr_sem)
@@ -254,9 +336,9 @@
                 ua[16:32, 128 * j:128 * j + 128] = jnp.where(left, swapped[2 * j], tiles[2 * j + 1]).astype(BF16)
             xv = dot(ua[...], tb[pl.ds(pl.multiple_of(c * 512, 512), 512), :])
             if n == 0:
-                xr[...] = xv
+                xv_[...] = xv
             else:
-                xr[...] += xv
+                xv_[...] += xv
         wait_sent(fsend, fs_sem)
 
         @pl.when(it == 0)
@@ -265,29 +347,37 @@
 
         for zz in range(8):
             cols = slice(256 * zz, 256 * zz + 256)
-            xv = xr[:, cols]
-            wx = wf[zz] * xv
+            xqn = xv_[:, cols] + beta * xq[:, cols]
+            xq[:, cols] = xqn
+            xn = xm[:, cols] - alpha * xqn
+            xm[:, cols] = xn
+            wx = wf[zz] * xn
             zb[:, cols] = wx.astype(BF16)
-            qa, qb = wx * xv, wx * xd[:, cols]
+            qa, qc = wx * xn, wx * xd[:, cols]
             suma += fold(qa[:, :128] + qa[:, 128:])
-            sumb += fold(qb[:, :128] + qb[:, 128:])
+            sumb += fold(qc[:, :128] + qc[:, 128:])
         row = lax.broadcasted_iota(jnp.int32, (8, 128), 0)
         one = [jnp.sum(part, axis=0, keepdims=True) for part in (norm, suma, sumb)]
         reduce_start(par, 0, jnp.where(row == 0, one[0], jnp.where(row == 1, one[1], one[2])))
         zv = zb[...]
-        for n, dy in enumerate(ROWS):
+        for dy in ROWS:
             c = (y + dy) % 4
-            v = dot(zv, tt4[c])
+            w = dot(zv, tt4[c])
             for j in range(4):
-                top, bottom = v[:16, 128 * j:128 * j + 128], v[16:, 128 * j:128 * j + 128]
+                top, bottom = w[:16, 128 * j:128 * j + 128], w[16:, 128 * j:128 * j + 128]
                 bsend[c * 8 + 2 * j] = jnp.where(left, top, swap(bottom)).astype(BF16)
                 bsend[c * 8 + 2 * j + 1] = jnp.where(left, swap(top), bottom).astype(BF16)
             send_row(dy, bsend, brecv, bs_sem, br_sem)
-            if n == 2:
-                part = reduce_finish(par, 0)
-                reduce_start(par, 1, part)
         brecv[p] = bsend[p]
         yacc[...] = dot(gt[...], pb[...])
+        part = reduce_finish(par, 0)
+        reduce_start(par, 1, part)
+
+        @pl.when(it > 0)
+        def _():
+            shipped(im, orecv.at[it - 1], or_sem.at[it - 1])
+            advance(orecv.at[it - 1], xb, rs)
+
         for dy in ROWS:
             c = (y + 4 - dy) % 4
             wait_row(dy, brecv, br_sem)
@@ -297,43 +387,12 @@
             vk[:, 1] = jnp.where(left, swapped, tiles).astype(BF16)
             yacc[...] += dot(s4[c], vk[...].reshape(256, 128))
         wait_sent(bsend, bs_sem)
-        sums = jnp.sum(reduce_finish(par, 1), axis=1, keepdims=True)
-        rr, ra, rb = sums[0:1], sums[1:2], sums[2:3]
-        beta = jnp.where(it == 0, 0.0, rr / scal[0, 0:1, 0:1])
-        curve = ra + beta * (2.0 * rb + beta * scal[1, 0:1, 0:1])
-        alpha = rr / curve
-        scal[0] = jnp.broadcast_to(rr, (8, 128))
-        scal[1] = jnp.broadcast_to(curve, (8, 128))
-        scal[2] = jnp.broadcast_to(beta, (8, 128))
         ya = yacc[...].reshape(8, 2, 64, 128)
-        qv = jnp.where(left, ya[:, 0], ya[:, 1]) + beta * q[...]
-        q[...] = qv
-        dv = r[...] + beta * d[...]
-        d[...] = dv
-        x_[...] += alpha * dv
-        r[...] -= alpha * qv
-
-    xv, rv = x_[...], r[...]
-    xs, rsw = swap(xv), swap(rv)
-    osend[:, 0:64] = jnp.where(left, xv, rsw).astype(BF16)
-    osend[:, 64:128] = jnp.where(left, xs, rv).astype(BF16)
-    slot_out = (z % 2) * 4 + x
-    for o in range(8):
-        zz = (z + o) % 8
-
-        def send():
-            remote(osend.at[zz], orecv.at[slot_out], os_sem.at[o], or_sem, dev(zz, m, z // 2)).start()
-        if o == 0:
-            pl.when(jnp.logical_not(home))(send)
-
-            @pl.when(home)
-            def _():
-                pltpu.make_async_copy(osend.at[zz], orecv.at[slot_out], or_sem).start()
-        else:
-            send()
-
-    def sent(src, sem):
-        remote(src, src, sem, sem, dev(z, m, x)).wait_send()
+        im[...] = jnp.where(left, ya[:, 0], ya[:, 1])
+
+    osend[...] = im[...].astype(BF16)
+    ship(osend, olast, or_sem.at[ITERS - 1])
+    scalars(ITERS - 1)
 
     for o in range(3):
         sent(isend.at[0], i1s.at[o])
@@ -349,20 +408,8 @@
         sent(w_cols.at[0], w1s.at[o - 1])
         sent(wf.at[0], w2s.at[o - 1])
 
-    pltpu.make_async_copy(orecv, orecv, or_sem).wait()
-    for e in range(2):
-        for h in range(2):
-            a = orecv[4 * e + 2 * h].astype(F32)
-            b = orecv[4 * e + 2 * h + 1].astype(F32)
-            xo_ref[e, :, 128 * h:128 * h + 128] = jnp.where(left, a, swap(b))
-            ro_ref[e, :, 128 * h:128 * h + 128] = jnp.where(left, swap(a), b)
-    for o in range(8):
-        if o == 0:
-            @pl.when(jnp.logical_not(home))
-            def _():
-                sent(osend.at[0], os_sem.at[o])
-        else:
-            sent(osend.at[0], os_sem.at[o])
+    shipped(osend, olast, or_sem.at[ITERS - 1])
+    advance(olast, xo_ref, ro_ref)
 
 
 def per_device(right_side, spatial_basis, temporal_basis, spectral_weight, pierce_nodes, pierce_weights):
@@ -388,11 +435,12 @@
         vm((8, 64, 128), F32),
         vm((8, 64, 128), F32),
         vm((8, 64, 128), F32),
-        vm((8, 64, 128), F32),
         vm((8, 2, 64, 128), BF16),
         vm((32, 16, 128), BF16),
         vm((32, 16, 128), BF16),
         vm((32, 512), BF16),
+        vm((32, 2048), F32),
+        vm((32, 2048), F32),
         vm((32, 2048), F32),
         vm((32, 2048), F32),
         vm((8, 32, 32), F32),
@@ -403,12 +451,17 @@
         vm((8, 2, 16, 128), BF16),
         vm((512, 128), F32),
         vm((512, 128), F32),
+        vm((512, 128), F32),
         vm((512, 128), BF16),
         vm((1024, 128), F32),
         vm((2, 2, 16, 8, 128), F32),
-        vm((3, 8, 128), F32),
-        vm((8, 128, 128), BF16),
-        vm((8, 128, 128), BF16),
+        vm((4, 8, 128), F32),
+        vm((2, 128, 256), F32),
+        vm((2, 128, 256), F32),
+        vm((2, 128, 256), F32),
+        vm((8, 64, 128), BF16),
+        vm((ITERS - 1, 8, 64, 128), F32),
+        vm((8, 64, 128), BF16),
         dma((9,)),
         dma((3,)),
         dma((3,)),
@@ -427,7 +480,7 @@
         dma((2, 2)),
         dma((2, 2)),
         dma((8,)),
-        dma,
+        dma((ITERS,)),
     ]
     out = jax.ShapeDtypeStruct(right_side.shape, F32)
     return pl.pallas_call(

time: 108 us -> 97.6 us (0.904)
  Pallas kernels: 103 us -> 93.1 us
    pallas_call x1, Pallas kernels: 103 us -> 93.1 us  [per_device(): pl.pallas_call(kernel, out_shape=(out, out), in_specs=[pl.BlockSpec(memor...]
where the time goes in v3:
time: 97.6 us; the launch traced here: 97.1 us
  Pallas kernels  93.1 us (95%)
  local copies, waits for them, and re-layouts  3.34 us (3%)
    pallas_call x1, Pallas kernels, per_device(): pl.pallas_call(kernel, out_shape=(out, out), in_specs=[pl.BlockSpec(memor...  93.1 us
    unnamed x2, local copies, waits for them, and re-layouts  3.34 us

profile of v3, /device:TPU:4, one launch (start us, length us, event | category | flops | bytes accessed | tf_op | source)
XLA Modules:
  0.0 97.1 jit_solution(11744094130965591935)
XLA Ops:
  0.6 93.1 %cg.1 = (f32[2,128,256]{2,1,0:T(8,128)}, f32[2,128,256]{2,1,0:T(8,128)}) custom-call(f32[2,128,256]{2,1,0:T(8,128)} %rs_hbm.1, bf16[1024,1024]{1,0:T(8,128)(2,1)} %s_hbm.1, bf16[2048,2048]{1,0:T(8,128)(2,1)} %t_hbm.1, f32[32,1024]{1,0:T(8,128)} %bitcast.1, s32[2,2,4,512]{3,2,1,0:T(4,128)} %pn_hbm.1, f32[2,2,4,512]{3,2,1,0:T(4,128)} %pw_hbm.1), custom_call_target="tpu_custom_call" | custom-call | tf_op jit(solution)/shard_map/cg/pallas_call | solution.py:486
  93.7 1.7 %copy.10 = f32[2,128,256]{2,1,0:T(8,128)} copy(f32[2,128,256]{2,1,0:T(8,128)} %get-tuple-element.4) | data formatting | bytes 524288
  95.4 1.7 %copy.11 = f32[2,128,256]{2,1,0:T(8,128)} copy(f32[2,128,256]{2,1,0:T(8,128)} %get-tuple-element.5) | data formatting | bytes 524288

commit v4 on v3

--- a/solution.py
+++ b/solution.py
@@ -9,7 +9,16 @@
 MESH = pl.DeviceIdType.MESH
 F32 = jnp.float32
 BF16 = jnp.bfloat16
-ROWS = (2, 1, 3, 0)
+
+
+def hops(dy, dx):
+    return min(dy, 4 - dy) + min(dx, 4 - dx)
+
+
+CHIPS = sorted(((dy, dx) for dy in range(4) for dx in range(4)), key=lambda o: (hops(*o), o))
+RANKS = [(dy, dc, dx) for dy, dx in CHIPS for dc in range(2)]
+BACK = [RANKS.index((-dy % 4, dc, -dx % 4)) for dy, dc, dx in RANKS]
+FAR_Z = (4, 3, 5, 2, 6, 1, 7)
 
 
 def dot(a, b):
@@ -32,9 +41,9 @@
 def kernel(
     rs_hbm, s_hbm, t_hbm, w_hbm, pn_hbm, pw_hbm,
     xo_ref, ro_ref,
-    rs, s4, st, tb, tt4, w_in, pn, pw, pnode, pwgt, g, gt,
+    rs, sn, s4, st, tb, tt4, w_in, pn, pw, pnode, pwgt, g, gt,
     w_cols, isend, i1, i2, im, r, q, vb, fsend, frecv, ua, xv_, xm, xq, xd, wslot, wf, zb, bsend, brecv, vk,
-    pr, pq, pd, pb, yacc, red, scal, xb, db, qb, osend, orecv, olast,
+    pr, pq, pd, pv_, pb, yacc, red, scal, xb, db, qb, osend, orecv, olast,
     load_sem, i1s, i1r, i2s, i2r, psend_sem, precv_sem, w1s, w1r, w2s, w2r,
     fs_sem, fr_sem, bs_sem, br_sem, rs_sem, rr_sem, os_sem, or_sem,
 ):
@@ -59,21 +68,29 @@
         pltpu.make_async_copy(pw_hbm, pw, load_sem.at[2]),
         pltpu.make_async_copy(w_hbm, w_in, load_sem.at[3]),
     ]
-    s_loads = [
-        pltpu.make_async_copy(s_hbm.at[:, pl.ds(256 * c, 256)], s4.at[c], load_sem.at[4 + c])
-        for c in range(4)
-    ]
-    t_load = pltpu.make_async_copy(t_hbm, tb, load_sem.at[8])
-    for copy in loads + s_loads + [t_load]:
+    s_load = pltpu.make_async_copy(s_hbm, sn, load_sem.at[4])
+
+    def peer(j):
+        dy, dc, dx = RANKS[j]
+        return 2 * ((y + dy) % 4) + (core + dc) % 2, (x + dx) % 4
+
+    def block(j):
+        mm, xx = peer(j)
+        return mm * 4 + xx
+
+    for copy in loads + [s_load]:
         copy.start()
+    for j in range(32):
+        rows = pl.ds(pl.multiple_of(block(j) * 64, 64), 64)
+        pltpu.make_async_copy(t_hbm.at[rows], tb.at[pl.ds(64 * j, 64)], load_sem.at[5]).start()
 
     barrier = pltpu.get_barrier_semaphore()
 
     def greet(to):
         pl.semaphore_signal(barrier, inc=1, device_id=to, device_id_type=MESH)
 
-    for o in range(1, 32):
-        greet(dev(z, (m + o // 4) % 8, (x + o % 4) % 4))
+    for j in range(1, 32):
+        greet(dev(z, *peer(j)))
     for o in range(2, 16):
         greet(dev((z + o // 2) % 8, 2 * y + (core + o) % 2, x))
     home = z // 2 == x
@@ -138,9 +155,13 @@
                 pltpu.make_async_copy(i1.at[zz], i2.at[z], i2r).start()
 
     forward(x)
+    s_load.wait()
+    s4[...] = sn[...].T.reshape(4, 256, 1024)
+    for j in range(32):
+        own = block(j)
+        st[32 * j:32 * j + 32, :] = s4[own // 8, pl.ds(pl.multiple_of(own % 8 * 32, 32), 32), :]
     for c in range(4):
-        s_loads[c].wait()
-        st[256 * c:256 * c + 256, :] = s4[c].T
+        sn[:, 256 * c:256 * c + 256] = st[256 * c:256 * c + 256, :].T
     for dx in (1, 3, 2):
         xx = (x + 4 - dx) % 4
         span = i1.at[pl.ds(2 * xx, 2)]
@@ -151,7 +172,7 @@
     own_w = wf.at[z]
     for h in range(2):
         own_w[:, 128 * h:128 * h + 128] = jnp.concatenate([wslot[4 * h + i] for i in range(4)], axis=1)
-    for o in range(1, 8):
+    for o in FAR_Z:
         remote(wf.at[z], wf.at[z], w2s.at[o - 1], w2r, dev((z + o) % 8, m, x)).start()
 
     for ref in (r, q, xm, xq, xd, pr, pq, pd, xb, db, qb):
@@ -183,8 +204,8 @@
             cols = pl.ds(pl.multiple_of(i * 256, 256), 256)
             tt4[c, cols, :] = tb[512 * c:512 * c + 512, cols].T
 
-    t_load.wait()
-    for c in range(2):
+    pltpu.make_async_copy(t_hbm, tb, load_sem.at[5]).wait()
+    for c in range(2, 4):
         transpose(c)
 
     pltpu.make_async_copy(i2, i2, i2r).wait()
@@ -194,12 +215,13 @@
         own = (y * 4 + x, z * 2 + core)[step]
         slot = red.at[par, step, own]
         slot[...] = value
-        for o in range(1, 16):
-            if step == 0:
-                where = dev(z, 2 * ((y + o // 4) % 4) + core, (x + o % 4) % 4)
-            else:
-                where = dev((z + o // 2) % 8, 2 * y + (core + o) % 2, x)
-            remote(slot, slot, rs_sem.at[par, step], rr_sem.at[par, step], where).start()
+        if step == 0:
+            where = [dev(z, 2 * ((y + dy) % 4) + core, (x + dx) % 4) for dy, dx in reversed(CHIPS[1:])]
+        else:
+            where = [dev((z + o) % 8, 2 * y + (core + dc) % 2, x) for o in FAR_Z for dc in range(2)]
+            where.append(dev(z, 2 * y + 1 - core, x))
+        for to in where:
+            remote(slot, slot, rs_sem.at[par, step], rr_sem.at[par, step], to).start()
 
     def reduce_finish(par, step):
         span = red.at[par, step, pl.ds(0, 15)]
@@ -208,18 +230,14 @@
         both.wait_send()
         return jnp.sum(red[par, step], axis=0)
 
-    def send_row(dy, src, dst, ssem, rsem):
-        c = (y + dy) % 4
-        for o in range(8):
-            if dy == 0 and o == 0:
-                continue
-            mm = 2 * c + (core + o // 4) % 2
-            xx = (x + o % 4) % 4
-            remote(src.at[mm * 4 + xx], dst.at[p], ssem, rsem.at[dy], dev(z, mm, xx)).start()
-
-    def wait_row(dy, buf, rsem):
-        span = buf.at[pl.ds(0, 7 if dy == 0 else 8)]
-        remote(span, span, rsem.at[dy], rsem.at[dy], dev(z, m, x)).wait_recv()
+    def send_group(c, src, dst, ssem, rsem):
+        for j in reversed(range(8 * c, 8 * c + 8)):
+            if j > 0:
+                remote(src.at[j], dst.at[BACK[j]], ssem, rsem.at[BACK[j] // 8], dev(z, *peer(j))).start()
+
+    def wait_group(c, buf, rsem):
+        span = buf.at[pl.ds(0, 7 if c == 0 else 8)]
+        remote(span, span, rsem.at[c], rsem.at[c], dev(z, m, x)).wait_recv()
 
     def wait_sent(buf, ssem):
         span = buf.at[pl.ds(0, 31)]
@@ -239,7 +257,7 @@
     slot_out = (z % 2) * 4 + x
 
     def ship(src, dst, sem):
-        for o in range(8):
+        for o in FAR_Z + (0,):
             zz = (z + o) % 8
 
             def send():
@@ -288,23 +306,39 @@
         vb[:, 0] = jnp.where(left, v, vsw).astype(BF16).reshape(8, 64, 128)
         vb[:, 1] = jnp.where(left, vsw, v).astype(BF16).reshape(8, 64, 128)
         vbv = vb[...].reshape(1024, 128)
-        for dy in ROWS:
-            c = (y + dy) % 4
-            u = dot(st[pl.ds(pl.multiple_of(c * 256, 256), 256), :], vbv).reshape(8, 2, 16, 128)
-            fsend[pl.ds(c * 8, 8)] = jnp.where(left, u[:, 0], u[:, 1]).astype(BF16)
-            send_row(dy, fsend, frecv, fs_sem, fr_sem)
-        frecv[p] = fsend[p]
+        for c in (3, 2, 1, 0):
+            u = dot(st[256 * c:256 * c + 256, :], vbv).reshape(8, 2, 16, 128)
+            fsend[8 * c:8 * c + 8] = jnp.where(left, u[:, 0], u[:, 1]).astype(BF16)
+            send_group(c, fsend, frecv, fs_sem, fr_sem)
+        frecv[0] = fsend[0]
 
         @pl.when(it == 0)
         def _():
-            for c in range(2, 4):
+            for c in range(2):
                 transpose(c)
 
         @pl.when(it > 0)
         def _():
-            ship(im, orecv.at[it - 1], or_sem.at[it - 1])
-
-        pv = dot(g[...], vbv)
+            osend[...] = im[...].astype(BF16)
+            ship(osend, orecv.at[it - 1], or_sem.at[it - 1])
+
+        pv_[...] = dot(g[...], vbv)
+
+        def modes(c):
+            wait_group(c, frecv, fr_sem)
+            tiles = frecv[8 * c:8 * c + 8].astype(F32)
+            swapped = swap(tiles)
+            for j in range(4):
+                ua[0:16, 128 * j:128 * j + 128] = jnp.where(left, tiles[2 * j], swapped[2 * j + 1]).astype(BF16)
+                ua[16:32, 128 * j:128 * j + 128] = jnp.where(left, swapped[2 * j], tiles[2 * j + 1]).astype(BF16)
+            xv = dot(ua[...], tb[512 * c:512 * c + 512, :])
+            if c == 0:
+                xv_[...] = xv
+            else:
+                xv_[...] += xv
+
+        modes(0)
+        modes(1)
 
         @pl.when(it > 0)
         def _():
@@ -313,7 +347,7 @@
         alpha, beta = factors()
         pold = pr[...] + beta * pd[...]
         pd[...] = pold
-        pqn = pv + beta * pq[...]
+        pqn = pv_[...] + beta * pq[...]
         pq[...] = pqn
         pnew = pr[...] - alpha * pqn
         pr[...] = pnew
@@ -326,19 +360,8 @@
         suma = 0.5 * fold(pnew * pnew)
         sumb = 0.5 * fold(pnew * pold)
         xd[...] = xm[...] + beta * xd[...]
-        for n, dy in enumerate(ROWS):
-            c = (y + 4 - dy) % 4
-            wait_row(dy, frecv, fr_sem)
-            tiles = frecv[pl.ds(c * 8, 8)].astype(F32)
-            swapped = swap(tiles)
-            for j in range(4):
-                ua[0:16, 128 * j:128 * j + 128] = jnp.where(left, tiles[2 * j], swapped[2 * j + 1]).astype(BF16)
-                ua[16:32, 128 * j:128 * j + 128] = jnp.where(left, swapped[2 * j], tiles[2 * j + 1]).astype(BF16)
-            xv = dot(ua[...], tb[pl.ds(pl.multiple_of(c * 512, 512), 512), :])
-            if n == 0:
-                xv_[...] = xv
-            else:
-                xv_[...] += xv
+        modes(2)
+        modes(3)
         wait_sent(fsend, fs_sem)
 
         @pl.when(it == 0)
@@ -360,32 +383,30 @@
         one = [jnp.sum(part, axis=0, keepdims=True) for part in (norm, suma, sumb)]
         reduce_start(par, 0, jnp.where(row == 0, one[0], jnp.where(row == 1, one[1], one[2])))
         zv = zb[...]
-        for dy in ROWS:
-            c = (y + dy) % 4
+        for c in (3, 2, 1, 0):
             w = dot(zv, tt4[c])
             for j in range(4):
                 top, bottom = w[:16, 128 * j:128 * j + 128], w[16:, 128 * j:128 * j + 128]
                 bsend[c * 8 + 2 * j] = jnp.where(left, top, swap(bottom)).astype(BF16)
                 bsend[c * 8 + 2 * j + 1] = jnp.where(left, swap(top), bottom).astype(BF16)
-            send_row(dy, bsend, brecv, bs_sem, br_sem)
-        brecv[p] = bsend[p]
+            send_group(c, bsend, brecv, bs_sem, br_sem)
+        brecv[0] = bsend[0]
         yacc[...] = dot(gt[...], pb[...])
+
+        @pl.when(it > 0)
+        def _():
+            shipped(osend, orecv.at[it - 1], or_sem.at[it - 1])
+            advance(orecv.at[it - 1], xb, rs)
+
         part = reduce_finish(par, 0)
         reduce_start(par, 1, part)
-
-        @pl.when(it > 0)
-        def _():
-            shipped(im, orecv.at[it - 1], or_sem.at[it - 1])
-            advance(orecv.at[it - 1], xb, rs)
-
-        for dy in ROWS:
-            c = (y + 4 - dy) % 4
-            wait_row(dy, brecv, br_sem)
-            tiles = brecv[pl.ds(c * 8, 8)].astype(F32)
+        for c in range(4):
+            wait_group(c, brecv, br_sem)
+            tiles = brecv[8 * c:8 * c + 8].astype(F32)
             swapped = swap(tiles)
             vk[:, 0] = jnp.where(left, tiles, swapped).astype(BF16)
             vk[:, 1] = jnp.where(left, swapped, tiles).astype(BF16)
-            yacc[...] += dot(s4[c], vk[...].reshape(256, 128))
+            yacc[...] += dot(sn[:, 256 * c:256 * c + 256], vk[...].reshape(256, 128))
         wait_sent(bsend, bs_sem)
         ya = yacc[...].reshape(8, 2, 64, 128)
         im[...] = jnp.where(left, ya[:, 0], ya[:, 1])
@@ -417,7 +438,8 @@
     dma = pltpu.SemaphoreType.DMA
     scratch = [
         vm((2, 128, 256), F32),
-        vm((4, 1024, 256), BF16),
+        vm((1024, 1024), BF16),
+        vm((4, 256, 1024), BF16),
         vm((1024, 1024), BF16),
         vm((2048, 2048), BF16),
         vm((4, 2048, 512), BF16),
@@ -452,6 +474,7 @@
         vm((512, 128), F32),
         vm((512, 128), F32),
         vm((512, 128), F32),
+        vm((512, 128), F32),
         vm((512, 128), BF16),
         vm((1024, 128), F32),
         vm((2, 2, 16, 8, 128), F32),
@@ -460,9 +483,9 @@
         vm((2, 128, 256), F32),
         vm((2, 128, 256), F32),
         vm((8, 64, 128), BF16),
-        vm((ITERS - 1, 8, 64, 128), F32),
+        vm((ITERS - 1, 8, 64, 128), BF16),
         vm((8, 64, 128), BF16),
-        dma((9,)),
+        dma((6,)),
         dma((3,)),
         dma((3,)),
         dma((7,)),

time: 97.6 us -> 93.2 us (0.955)
  Pallas kernels: 93.1 us -> 88.3 us
    pallas_call x1, Pallas kernels: 93.1 us -> 88.3 us  [per_device(): pl.pallas_call(kernel, out_shape=(out, out), in_specs=[pl.BlockSpec(memor...]
where the time goes in v4:
time: 93.2 us; the launch traced here: 92.3 us
  Pallas kernels  88.3 us (95%)
  local copies, waits for them, and re-layouts  3.34 us (4%)
    pallas_call x1, Pallas kernels, per_device(): pl.pallas_call(kernel, out_shape=(out, out), in_specs=[pl.BlockSpec(memor...  88.3 us
    unnamed x2, local copies, waits for them, and re-layouts  3.34 us

profile of v4, /device:TPU:4, one launch (start us, length us, event | category | flops | bytes accessed | tf_op | source)
XLA Modules:
  0.0 92.3 jit_solution(4302006480824859195)
XLA Ops:
  0.6 88.3 %cg.1 = (f32[2,128,256]{2,1,0:T(8,128)}, f32[2,128,256]{2,1,0:T(8,128)}) custom-call(f32[2,128,256]{2,1,0:T(8,128)} %rs_hbm.1, bf16[1024,1024]{1,0:T(8,128)(2,1)} %s_hbm.1, bf16[2048,2048]{1,0:T(8,128)(2,1)} %t_hbm.1, f32[32,1024]{1,0:T(8,128)} %bitcast.1, s32[2,2,4,512]{3,2,1,0:T(4,128)} %pn_hbm.1, f32[2,2,4,512]{3,2,1,0:T(4,128)} %pw_hbm.1), custom_call_target="tpu_custom_call" | custom-call | tf_op jit(solution)/shard_map/cg/pallas_call | solution.py:509
  88.9 1.7 %copy.10 = f32[2,128,256]{2,1,0:T(8,128)} copy(f32[2,128,256]{2,1,0:T(8,128)} %get-tuple-element.4) | data formatting | bytes 524288
  90.6 1.7 %copy.11 = f32[2,128,256]{2,1,0:T(8,128)} copy(f32[2,128,256]{2,1,0:T(8,128)} %get-tuple-element.5) | data formatting | bytes 524288

commit v5 on v4

--- a/solution.py
+++ b/solution.py
@@ -19,6 +19,12 @@
 RANKS = [(dy, dc, dx) for dy, dx in CHIPS for dc in range(2)]
 BACK = [RANKS.index((-dy % 4, dc, -dx % 4)) for dy, dc, dx in RANKS]
 FAR_Z = (4, 3, 5, 2, 6, 1, 7)
+FWD_SEND, FWD_WAIT = ((24, 32), (16, 24), (8, 16), (0, 8)), ((0, 8), (8, 16), (16, 24), (24, 32))
+BACK_SEND, BACK_WAIT = FWD_SEND, FWD_WAIT
+
+
+def group_of(groups, rank):
+    return [a <= rank < b for a, b in groups].index(True)
 
 
 def dot(a, b):
@@ -41,7 +47,7 @@
 def kernel(
     rs_hbm, s_hbm, t_hbm, w_hbm, pn_hbm, pw_hbm,
     xo_ref, ro_ref,
-    rs, sn, s4, st, tb, tt4, w_in, pn, pw, pnode, pwgt, g, gt,
+    rs, sn, s4, st, tb, tt, w_in, pn, pw, pnode, pwgt, g, gt,
     w_cols, isend, i1, i2, im, r, q, vb, fsend, frecv, ua, xv_, xm, xq, xd, wslot, wf, zb, bsend, brecv, vk,
     pr, pq, pd, pv_, pb, yacc, red, scal, xb, db, qb, osend, orecv, olast,
     load_sem, i1s, i1r, i2s, i2r, psend_sem, precv_sem, w1s, w1r, w2s, w2r,
@@ -53,6 +59,7 @@
     y, core = m // 2, m % 2
     p = m * 4 + x
     left = lax.broadcasted_iota(jnp.int32, (1, 128), 1) < 64
+    home = z // 2 == x
 
     def dev(zz, mm, xx):
         return {"space": zz, "tm": mm, "dir": xx}
@@ -61,6 +68,21 @@
         return pltpu.make_async_remote_copy(
             src_ref=src, dst_ref=dst, send_sem=ss, recv_sem=rsem, device_id=to, device_id_type=MESH
         )
+
+    def peer(j):
+        dy, dc, dx = RANKS[j]
+        return 2 * ((y + dy) % 4) + (core + dc) % 2, (x + dx) % 4
+
+    barrier = pltpu.get_barrier_semaphore()
+
+    def greet(to):
+        pl.semaphore_signal(barrier, inc=1, device_id=to, device_id_type=MESH)
+
+    for o in FAR_Z:
+        for dc in range(2):
+            greet(dev((z + o) % 8, 2 * y + (core + dc) % 2, x))
+    for j in reversed(range(1, 32)):
+        greet(dev(z, *peer(j)))
 
     loads = [
         pltpu.make_async_copy(rs_hbm, rs, load_sem.at[0]),
@@ -70,10 +92,6 @@
     ]
     s_load = pltpu.make_async_copy(s_hbm, sn, load_sem.at[4])
 
-    def peer(j):
-        dy, dc, dx = RANKS[j]
-        return 2 * ((y + dy) % 4) + (core + dc) % 2, (x + dx) % 4
-
     def block(j):
         mm, xx = peer(j)
         return mm * 4 + xx
@@ -83,32 +101,6 @@
     for j in range(32):
         rows = pl.ds(pl.multiple_of(block(j) * 64, 64), 64)
         pltpu.make_async_copy(t_hbm.at[rows], tb.at[pl.ds(64 * j, 64)], load_sem.at[5]).start()
-
-    barrier = pltpu.get_barrier_semaphore()
-
-    def greet(to):
-        pl.semaphore_signal(barrier, inc=1, device_id=to, device_id_type=MESH)
-
-    for j in range(1, 32):
-        greet(dev(z, *peer(j)))
-    for o in range(2, 16):
-        greet(dev((z + o // 2) % 8, 2 * y + (core + o) % 2, x))
-    home = z // 2 == x
-    for e in range(2):
-        for dx in range(4):
-            if dx == 0:
-                @pl.when(z != 2 * x + e)
-                def _():
-                    greet(dev(2 * x + e, m, x))
-            else:
-                greet(dev(2 * x + e, m, (x + dx) % 4))
-    for o in range(8):
-        if o == 0:
-            @pl.when(jnp.logical_not(home))
-            def _():
-                greet(dev(z, m, z // 2))
-        else:
-            greet(dev((z + o) % 8, m, z // 2))
 
     loads[0].wait()
     for h in range(2):
@@ -122,7 +114,7 @@
         copy.wait()
     w_cols[...] = w_in[...].T.reshape(32, 32, 32)
 
-    pl.semaphore_wait(barrier, 61 - 2 * home.astype(jnp.int32))
+    pl.semaphore_wait(barrier, 45)
 
     for dx in (2, 1, 3):
         xx = (x + dx) % 4
@@ -202,14 +194,18 @@
         @pl.loop(0, 8)
         def _(i):
             cols = pl.ds(pl.multiple_of(i * 256, 256), 256)
-            tt4[c, cols, :] = tb[512 * c:512 * c + 512, cols].T
+            tt[cols, 512 * c:512 * c + 512] = tb[512 * c:512 * c + 512, cols].T
 
     pltpu.make_async_copy(t_hbm, tb, load_sem.at[5]).wait()
     for c in range(2, 4):
         transpose(c)
 
     pltpu.make_async_copy(i2, i2, i2r).wait()
-    im[...] = i2[...].astype(F32)
+    first = i2[...].astype(F32)
+    turned = swap(first)
+    im[...] = first
+    vb[:, 0] = jnp.where(left, first, turned).astype(BF16)
+    vb[:, 1] = jnp.where(left, turned, first).astype(BF16)
 
     def reduce_start(par, step, value):
         own = (y * 4 + x, z * 2 + core)[step]
@@ -230,14 +226,17 @@
         both.wait_send()
         return jnp.sum(red[par, step], axis=0)
 
-    def send_group(c, src, dst, ssem, rsem):
-        for j in reversed(range(8 * c, 8 * c + 8)):
+    def send_group(ranks, groups, src, dst, ssem, rsem):
+        for j in reversed(range(*ranks)):
             if j > 0:
-                remote(src.at[j], dst.at[BACK[j]], ssem, rsem.at[BACK[j] // 8], dev(z, *peer(j))).start()
-
-    def wait_group(c, buf, rsem):
-        span = buf.at[pl.ds(0, 7 if c == 0 else 8)]
-        remote(span, span, rsem.at[c], rsem.at[c], dev(z, m, x)).wait_recv()
+                sem = rsem.at[group_of(groups, BACK[j])]
+                remote(src.at[j], dst.at[BACK[j]], ssem, sem, dev(z, *peer(j))).start()
+
+    def wait_group(ranks, groups, buf, rsem):
+        a, b = ranks
+        span = buf.at[pl.ds(0, b - max(a, 1))]
+        sem = rsem.at[groups.index(ranks)]
+        remote(span, span, sem, sem, dev(z, m, x)).wait_recv()
 
     def wait_sent(buf, ssem):
         span = buf.at[pl.ds(0, 31)]
@@ -301,15 +300,11 @@
     @pl.loop(0, ITERS)
     def _(it):
         par = it % 2
-        v = im[...].reshape(512, 128)
-        vsw = swap(v)
-        vb[:, 0] = jnp.where(left, v, vsw).astype(BF16).reshape(8, 64, 128)
-        vb[:, 1] = jnp.where(left, vsw, v).astype(BF16).reshape(8, 64, 128)
         vbv = vb[...].reshape(1024, 128)
-        for c in (3, 2, 1, 0):
-            u = dot(st[256 * c:256 * c + 256, :], vbv).reshape(8, 2, 16, 128)
-            fsend[8 * c:8 * c + 8] = jnp.where(left, u[:, 0], u[:, 1]).astype(BF16)
-            send_group(c, fsend, frecv, fs_sem, fr_sem)
+        for a, b in FWD_SEND:
+            u = dot(st[32 * a:32 * b, :], vbv).reshape(b - a, 2, 16, 128)
+            fsend[a:b] = jnp.where(left, u[:, 0], u[:, 1]).astype(BF16)
+            send_group((a, b), FWD_WAIT, fsend, frecv, fs_sem, fr_sem)
         frecv[0] = fsend[0]
 
         @pl.when(it == 0)
@@ -323,22 +318,24 @@
             ship(osend, orecv.at[it - 1], or_sem.at[it - 1])
 
         pv_[...] = dot(g[...], vbv)
-
-        def modes(c):
-            wait_group(c, frecv, fr_sem)
-            tiles = frecv[8 * c:8 * c + 8].astype(F32)
+        v = im[...].reshape(512, 128)
+
+        def modes(ranks):
+            a, b = ranks
+            wait_group(ranks, FWD_WAIT, frecv, fr_sem)
+            tiles = frecv[a:b].astype(F32)
             swapped = swap(tiles)
-            for j in range(4):
+            for j in range((b - a) // 2):
                 ua[0:16, 128 * j:128 * j + 128] = jnp.where(left, tiles[2 * j], swapped[2 * j + 1]).astype(BF16)
                 ua[16:32, 128 * j:128 * j + 128] = jnp.where(left, swapped[2 * j], tiles[2 * j + 1]).astype(BF16)
-            xv = dot(ua[...], tb[512 * c:512 * c + 512, :])
-            if c == 0:
+            xv = dot(ua[:, :64 * (b - a)], tb[64 * a:64 * b, :])
+            if ranks == FWD_WAIT[0]:
                 xv_[...] = xv
             else:
                 xv_[...] += xv
 
-        modes(0)
-        modes(1)
+        for ranks in FWD_WAIT[:-1]:
+            modes(ranks)
 
         @pl.when(it > 0)
         def _():
@@ -360,8 +357,7 @@
         suma = 0.5 * fold(pnew * pnew)
         sumb = 0.5 * fold(pnew * pold)
         xd[...] = xm[...] + beta * xd[...]
-        modes(2)
-        modes(3)
+        modes(FWD_WAIT[-1])
         wait_sent(fsend, fs_sem)
 
         @pl.when(it == 0)
@@ -383,13 +379,13 @@
         one = [jnp.sum(part, axis=0, keepdims=True) for part in (norm, suma, sumb)]
         reduce_start(par, 0, jnp.where(row == 0, one[0], jnp.where(row == 1, one[1], one[2])))
         zv = zb[...]
-        for c in (3, 2, 1, 0):
-            w = dot(zv, tt4[c])
-            for j in range(4):
+        for a, b in BACK_SEND:
+            w = dot(zv, tt[:, 64 * a:64 * b])
+            for j in range((b - a) // 2):
                 top, bottom = w[:16, 128 * j:128 * j + 128], w[16:, 128 * j:128 * j + 128]
-                bsend[c * 8 + 2 * j] = jnp.where(left, top, swap(bottom)).astype(BF16)
-                bsend[c * 8 + 2 * j + 1] = jnp.where(left, swap(top), bottom).astype(BF16)
-            send_group(c, bsend, brecv, bs_sem, br_sem)
+                bsend[a + 2 * j] = jnp.where(left, top, swap(bottom)).astype(BF16)
+                bsend[a + 2 * j + 1] = jnp.where(left, swap(top), bottom).astype(BF16)
+            send_group((a, b), BACK_WAIT, bsend, brecv, bs_sem, br_sem)
         brecv[0] = bsend[0]
         yacc[...] = dot(gt[...], pb[...])
 
@@ -400,15 +396,19 @@
 
         part = reduce_finish(par, 0)
         reduce_start(par, 1, part)
-        for c in range(4):
-            wait_group(c, brecv, br_sem)
-            tiles = brecv[8 * c:8 * c + 8].astype(F32)
+        for ranks in BACK_WAIT:
+            a, b = ranks
+            wait_group(ranks, BACK_WAIT, brecv, br_sem)
+            tiles = brecv[a:b].astype(F32)
             swapped = swap(tiles)
-            vk[:, 0] = jnp.where(left, tiles, swapped).astype(BF16)
-            vk[:, 1] = jnp.where(left, swapped, tiles).astype(BF16)
-            yacc[...] += dot(sn[:, 256 * c:256 * c + 256], vk[...].reshape(256, 128))
+            vk[a:b, 0] = jnp.where(left, tiles, swapped).astype(BF16)
+            vk[a:b, 1] = jnp.where(left, swapped, tiles).astype(BF16)
+            part = yacc[...] + dot(sn[:, 32 * a:32 * b], vk[a:b].reshape(32 * (b - a), 128))
+            if ranks != BACK_WAIT[-1]:
+                yacc[...] = part
         wait_sent(bsend, bs_sem)
-        ya = yacc[...].reshape(8, 2, 64, 128)
+        ya = part.reshape(8, 2, 64, 128)
+        vb[...] = ya.astype(BF16)
         im[...] = jnp.where(left, ya[:, 0], ya[:, 1])
 
     osend[...] = im[...].astype(BF16)
@@ -431,6 +431,11 @@
 
     shipped(osend, olast, or_sem.at[ITERS - 1])
     advance(olast, xo_ref, ro_ref)
+
+
+def hand_over(x_in, r_in, x_out, r_out):
+    x_out[...] = x_in[...]
+    r_out[...] = r_in[...]
 
 
 def per_device(right_side, spatial_basis, temporal_basis, spectral_weight, pierce_nodes, pierce_weights):
@@ -442,7 +447,7 @@
         vm((4, 256, 1024), BF16),
         vm((1024, 1024), BF16),
         vm((2048, 2048), BF16),
-        vm((4, 2048, 512), BF16),
+        vm((2048, 2048), BF16),
         vm((32, 1024), F32),
         vm((2, 2, 4, 512), jnp.int32),
         vm((2, 2, 4, 512), F32),
@@ -460,7 +465,7 @@
         vm((8, 2, 64, 128), BF16),
         vm((32, 16, 128), BF16),
         vm((32, 16, 128), BF16),
-        vm((32, 512), BF16),
+        vm((32, 2048), BF16),
         vm((32, 2048), F32),
         vm((32, 2048), F32),
         vm((32, 2048), F32),
@@ -470,7 +475,7 @@
         vm((32, 2048), BF16),
         vm((32, 16, 128), BF16),
         vm((32, 16, 128), BF16),
-        vm((8, 2, 16, 128), BF16),
+        vm((32, 2, 16, 128), BF16),
         vm((512, 128), F32),
         vm((512, 128), F32),
         vm((512, 128), F32),
@@ -506,7 +511,7 @@
         dma((ITERS,)),
     ]
     out = jax.ShapeDtypeStruct(right_side.shape, F32)
-    return pl.pallas_call(
+    results = pl.pallas_call(
         kernel,
         out_shape=(out, out),
         in_specs=[pl.BlockSpec(memory_space=pl.ANY)] * 6,
@@ -517,6 +522,14 @@
             collective_id=0, has_side_effects=True, vmem_limit_bytes=56 * 2**20
         ),
     )(right_side, spatial_basis, temporal_basis, spectral_weight.T, pierce_nodes, pierce_weights)
+    whole = (pl.BlockSpec(memory_space=vm),) * 2
+    return pl.pallas_call(
+        hand_over,
+        out_shape=(out, out),
+        in_specs=whole,
+        out_specs=whole,
+        name="hand_over",
+    )(*results)
 
 
 def solution(mesh):

time: 93.2 us -> 92.2 us (0.989)
  local copies, waits for them, and re-layouts: 3.34 us -> 0 us
  Pallas kernels: 88.3 us -> 89.9 us
    unnamed x2 -> x0, local copies, waits for them, and re-layouts: 3.34 us -> none
    pallas_call x0 -> x1, Pallas kernels: none -> 1.84 us  [per_device(): pl.pallas_call(hand_over, out_shape=(out, out), in_specs=whole, out_specs...]
where the time goes in v5:
time: 92.2 us; the launch traced here: 90.5 us
  Pallas kernels  89.9 us (98%)
    pallas_call x1, Pallas kernels, per_device(): pl.pallas_call(kernel, out_shape=(out, out), in_specs=[pl.BlockSpec(memor...  88 us

profile of v5, /device:TPU:4, one launch (start us, length us, event | category | flops | bytes accessed | tf_op | source)
XLA Modules:
  0.0 90.5 jit_solution(10727361180774312095)
XLA Ops:
  0.6 88.0 %cg.1 = (f32[2,128,256]{2,1,0:T(8,128)}, f32[2,128,256]{2,1,0:T(8,128)}) custom-call(f32[2,128,256]{2,1,0:T(8,128)} %rs_hbm.1, bf16[1024,1024]{1,0:T(8,128)(2,1)} %s_hbm.1, bf16[2048,2048]{1,0:T(8,128)(2,1)} %t_hbm.1, f32[32,1024]{1,0:T(8,128)} %bitcast.1, s32[2,2,4,512]{3,2,1,0:T(4,128)} %pn_hbm.1, f32[2,2,4,512]{3,2,1,0:T(4,128)} %pw_hbm.1), custom_call_target="tpu_custom_call" | custom-call | tf_op jit(solution)/shard_map/cg/pallas_call | solution.py:514
  88.7 1.8 %hand_over.1 = (f32[2,128,256]{2,1,0:T(8,128)}, f32[2,128,256]{2,1,0:T(8,128)}) custom-call(f32[2,128,256]{2,1,0:T(8,128)} %get-tuple-element.4.x_in, f32[2,128,256]{2,1,0:T(8,128)} %get-tuple-element.5.r_in), custom_call_target="tpu_custom_call" | custom-call | tf_op jit(solution)/shard_map/hand_over/pallas_call | solution.py:526

commit v6 on v5

--- a/solution.py
+++ b/solution.py
@@ -283,7 +283,7 @@
     def sent(src, sem):
         remote(src, src, sem, sem, dev(z, m, x)).wait_send()
 
-    def advance(tiles, x_out, r_out):
+    def advance(tiles):
         alpha, beta = factors()
         for e in range(2):
             for h in range(2):
@@ -294,8 +294,8 @@
                     dn = rs[at] + beta * db[at]
                     qb[at] = qn
                     db[at] = dn
-                    x_out[at] = xb[at] + alpha * dn
-                    r_out[at] = rs[at] - alpha * qn
+                    xb[at] += alpha * dn
+                    rs[at] -= alpha * qn
 
     @pl.loop(0, ITERS)
     def _(it):
@@ -333,9 +333,6 @@
                 xv_[...] = xv
             else:
                 xv_[...] += xv
-
-        for ranks in FWD_WAIT[:-1]:
-            modes(ranks)
 
         @pl.when(it > 0)
         def _():
@@ -357,7 +354,8 @@
         suma = 0.5 * fold(pnew * pnew)
         sumb = 0.5 * fold(pnew * pold)
         xd[...] = xm[...] + beta * xd[...]
-        modes(FWD_WAIT[-1])
+        for ranks in FWD_WAIT:
+            modes(ranks)
         wait_sent(fsend, fs_sem)
 
         @pl.when(it == 0)
@@ -392,7 +390,7 @@
         @pl.when(it > 0)
         def _():
             shipped(osend, orecv.at[it - 1], or_sem.at[it - 1])
-            advance(orecv.at[it - 1], xb, rs)
+            advance(orecv.at[it - 1])
 
         part = reduce_finish(par, 0)
         reduce_start(par, 1, part)
@@ -414,6 +412,9 @@
     osend[...] = im[...].astype(BF16)
     ship(osend, olast, or_sem.at[ITERS - 1])
     scalars(ITERS - 1)
+    alpha, beta = factors()
+    xo_ref[...] = xb[...] + alpha * (rs[...] + beta * db[...])
+    rs[...] = rs[...] - (alpha * beta) * qb[...]
 
     for o in range(3):
         sent(isend.at[0], i1s.at[o])
@@ -430,12 +431,25 @@
         sent(wf.at[0], w2s.at[o - 1])
 
     shipped(osend, olast, or_sem.at[ITERS - 1])
-    advance(olast, xo_ref, ro_ref)
-
-
-def hand_over(x_in, r_in, x_out, r_out):
-    x_out[...] = x_in[...]
-    r_out[...] = r_in[...]
+    for e in range(2):
+        for h in range(2):
+            a, b = olast[4 * e + 2 * h].astype(F32), olast[4 * e + 2 * h + 1].astype(F32)
+            cols = slice(128 * h, 128 * h + 128)
+            ro_ref[e, 0:64, cols] = rs[e, 0:64, cols] - alpha * jnp.where(left, a, swap(b))
+            ro_ref[e, 64:128, cols] = rs[e, 64:128, cols] - alpha * jnp.where(left, swap(a), b)
+
+
+def hand_over(x_in, r_in, x_out, r_out, x_held, r_held, sem):
+    steps = ((x_in, x_held, x_out), (r_in, r_held, r_out))
+    ins = [pltpu.make_async_copy(a, held, sem.at[n]) for n, (a, held, b) in enumerate(steps)]
+    outs = [pltpu.make_async_copy(held, b, sem.at[2 + n]) for n, (a, held, b) in enumerate(steps)]
+    for copy in ins:
+        copy.start()
+    for arrived, copy in zip(ins, outs):
+        arrived.wait()
+        copy.start()
+    for copy in outs:
+        copy.wait()
 
 
 def per_device(right_side, spatial_basis, temporal_basis, spectral_weight, pierce_nodes, pierce_weights):
@@ -522,12 +536,14 @@
             collective_id=0, has_side_effects=True, vmem_limit_bytes=56 * 2**20
         ),
     )(right_side, spatial_basis, temporal_basis, spectral_weight.T, pierce_nodes, pierce_weights)
-    whole = (pl.BlockSpec(memory_space=vm),) * 2
+    anywhere = (pl.BlockSpec(memory_space=pl.ANY),) * 2
     return pl.pallas_call(
         hand_over,
         out_shape=(out, out),
-        in_specs=whole,
-        out_specs=whole,
+        in_specs=anywhere,
+        out_specs=anywhere,
+        scratch_shapes=[vm(right_side.shape, F32)] * 2 + [dma((4,))],
+        compiler_params=pltpu.CompilerParams(vmem_limit_bytes=60 * 2**20),
         name="hand_over",
     )(*results)
 

time: 92.2 us -> 90.9 us (0.986)
  no operation moved by 1% of the time
where the time goes in v6:
time: 90.9 us; the launch traced here: 89.8 us
  Pallas kernels  89.1 us (98%)
    pallas_call x1, Pallas kernels, per_device(): pl.pallas_call(kernel, out_shape=(out, out), in_specs=[pl.BlockSpec(memor...  87.3 us

profile of v6, /device:TPU:4, one launch (start us, length us, event | category | flops | bytes accessed | tf_op | source)
XLA Modules:
  0.0 89.8 jit_solution(15284662828218819)
XLA Ops:
  0.6 87.3 %cg.1 = (f32[2,128,256]{2,1,0:T(8,128)}, f32[2,128,256]{2,1,0:T(8,128)}) custom-call(f32[2,128,256]{2,1,0:T(8,128)} %rs_hbm.1, bf16[1024,1024]{1,0:T(8,128)(2,1)} %s_hbm.1, bf16[2048,2048]{1,0:T(8,128)(2,1)} %t_hbm.1, f32[32,1024]{1,0:T(8,128)} %bitcast.1, s32[2,2,4,512]{3,2,1,0:T(4,128)} %pn_hbm.1, f32[2,2,4,512]{3,2,1,0:T(4,128)} %pw_hbm.1), custom_call_target="tpu_custom_call" | custom-call | tf_op jit(solution)/shard_map/cg/pallas_call | solution.py:528
  88.0 1.8 %hand_over.1 = (f32[2,128,256]{2,1,0:T(8,128)}, f32[2,128,256]{2,1,0:T(8,128)}) custom-call(f32[2,128,256]{2,1,0:T(8,128)} %get-tuple-element.4.x_in, f32[2,128,256]{2,1,0:T(8,128)} %get-tuple-element.5.r_in), custom_call_target="tpu_custom_call" | custom-call | tf_op jit(solution)/shard_map/hand_over/pallas_call | solution.py:540

commit v7 on v6

--- a/solution.py
+++ b/solution.py
@@ -112,7 +112,7 @@
     i1[pl.ds(2 * x, 2)] = isend[x]
     for copy in loads[1:]:
         copy.wait()
-    w_cols[...] = w_in[...].T.reshape(32, 32, 32)
+    w_cols[...] = w_in[...].T.reshape(32, 32, 32).astype(BF16)
 
     pl.semaphore_wait(barrier, 45)
 
@@ -163,9 +163,7 @@
     pltpu.make_async_copy(wslot, wslot, w1r).wait()
     own_w = wf.at[z]
     for h in range(2):
-        own_w[:, 128 * h:128 * h + 128] = jnp.concatenate([wslot[4 * h + i] for i in range(4)], axis=1)
-    for o in FAR_Z:
-        remote(wf.at[z], wf.at[z], w2s.at[o - 1], w2r, dev((z + o) % 8, m, x)).start()
+        own_w[:, 128 * h:128 * h + 128] = jnp.concatenate([wslot[4 * h + i].astype(F32) for i in range(4)], axis=1).astype(BF16)
 
     for ref in (r, q, xm, xq, xd, pr, pq, pd, xb, db, qb):
         ref[...] = jnp.zeros_like(ref)
@@ -201,6 +199,8 @@
         transpose(c)
 
     pltpu.make_async_copy(i2, i2, i2r).wait()
+    for o in FAR_Z:
+        remote(wf.at[z], wf.at[z], w2s.at[o - 1], w2r, dev((z + o) % 8, m, x)).start()
     first = i2[...].astype(F32)
     turned = swap(first)
     im[...] = first
@@ -368,7 +368,7 @@
             xq[:, cols] = xqn
             xn = xm[:, cols] - alpha * xqn
             xm[:, cols] = xn
-            wx = wf[zz] * xn
+            wx = wf[zz].astype(F32) * xn
             zb[:, cols] = wx.astype(BF16)
             qa, qc = wx * xn, wx * xd[:, cols]
             suma += fold(qa[:, :128] + qa[:, 128:])
@@ -469,7 +469,7 @@
         vm((4, 512), F32),
         vm((512, 1024), BF16),
         vm((1024, 512), BF16),
-        vm((32, 32, 32), F32),
+        vm((32, 32, 32), BF16),
         vm((4, 2, 64, 128), BF16),
         vm((8, 64, 128), BF16),
         vm((8, 64, 128), BF16),
@@ -484,8 +484,8 @@
         vm((32, 2048), F32),
         vm((32, 2048), F32),
         vm((32, 2048), F32),
-        vm((8, 32, 32), F32),
-        vm((8, 32, 256), F32),
+        vm((8, 32, 32), BF16),
+        vm((8, 32, 256), BF16),
         vm((32, 2048), BF16),
         vm((32, 16, 128), BF16),
         vm((32, 16, 128), BF16),

time: 90.9 us -> 87.1 us (0.958)
  the two profiles are of different devices: /device:TPU:4 before, /device:TPU:1 now
where the time goes in v7:
time: 87.1 us; the launch traced here: 87 us
  Pallas kernels  86.4 us (99%)
    pallas_call x1, Pallas kernels, per_device(): pl.pallas_call(kernel, out_shape=(out, out), in_specs=[pl.BlockSpec(memor...  84.6 us
    pallas_call x1, Pallas kernels, per_device(): pl.pallas_call(hand_over, out_shape=(out, out), in_specs=anywhere, out_sp...  1.77 us

profile of v7, /device:TPU:1, one launch (start us, length us, event | category | flops | bytes accessed | tf_op | source)
XLA Modules:
  0.0 87.0 jit_solution(7014989100562028121)
XLA Ops:
  0.6 84.6 %cg.1 = (f32[2,128,256]{2,1,0:T(8,128)}, f32[2,128,256]{2,1,0:T(8,128)}) custom-call(f32[2,128,256]{2,1,0:T(8,128)} %rs_hbm.1, bf16[1024,1024]{1,0:T(8,128)(2,1)} %s_hbm.1, bf16[2048,2048]{1,0:T(8,128)(2,1)} %t_hbm.1, f32[32,1024]{1,0:T(8,128)} %bitcast.1, s32[2,2,4,512]{3,2,1,0:T(4,128)} %pn_hbm.1, f32[2,2,4,512]{3,2,1,0:T(4,128)} %pw_hbm.1), custom_call_target="tpu_custom_call" | custom-call | tf_op jit(solution)/shard_map/cg/pallas_call | solution.py:528
  85.2 1.8 %hand_over.1 = (f32[2,128,256]{2,1,0:T(8,128)}, f32[2,128,256]{2,1,0:T(8,128)}) custom-call(f32[2,128,256]{2,1,0:T(8,128)} %get-tuple-element.4.x_in, f32[2,128,256]{2,1,0:T(8,128)} %get-tuple-element.5.r_in), custom_call_target="tpu_custom_call" | custom-call | tf_op jit(solution)/shard_map/hand_over/pallas_call | solution.py:540

commit v8 on v7

--- a/solution.py
+++ b/solution.py
@@ -79,10 +79,11 @@
         pl.semaphore_signal(barrier, inc=1, device_id=to, device_id_type=MESH)
 
     for o in FAR_Z:
-        for dc in range(2):
-            greet(dev((z + o) % 8, 2 * y + (core + dc) % 2, x))
-    for j in reversed(range(1, 32)):
-        greet(dev(z, *peer(j)))
+        greet(dev((z + o) % 8, m, x))
+    for o in range(1, 8):
+        greet(dev(z, (m + o) % 8, x))
+    for o in (2, 1, 3):
+        greet(dev(z, m, (x + o) % 4))
 
     loads = [
         pltpu.make_async_copy(rs_hbm, rs, load_sem.at[0]),
@@ -114,7 +115,7 @@
         copy.wait()
     w_cols[...] = w_in[...].T.reshape(32, 32, 32).astype(BF16)
 
-    pl.semaphore_wait(barrier, 45)
+    pl.semaphore_wait(barrier, 17)
 
     for dx in (2, 1, 3):
         xx = (x + dx) % 4

time: 87.1 us -> 86.1 us (0.989)
  the two profiles are of different devices: /device:TPU:1 before, /device:TPU:4 now
where the time goes in v8:
time: 86.1 us; the launch traced here: 84.7 us
  Pallas kernels  84 us (98%)
    pallas_call x1, Pallas kernels, per_device(): pl.pallas_call(kernel, out_shape=(out, out), in_specs=[pl.BlockSpec(memor...  82.3 us
    pallas_call x1, Pallas kernels, per_device(): pl.pallas_call(hand_over, out_shape=(out, out), in_specs=anywhere, out_sp...  1.77 us

profile of v8, /device:TPU:4, one launch (start us, length us, event | category | flops | bytes accessed | tf_op | source)
XLA Modules:
  0.0 84.7 jit_solution(1061804485710868758)
XLA Ops:
  0.6 82.3 %cg.1 = (f32[2,128,256]{2,1,0:T(8,128)}, f32[2,128,256]{2,1,0:T(8,128)}) custom-call(f32[2,128,256]{2,1,0:T(8,128)} %rs_hbm.1, bf16[1024,1024]{1,0:T(8,128)(2,1)} %s_hbm.1, bf16[2048,2048]{1,0:T(8,128)(2,1)} %t_hbm.1, f32[32,1024]{1,0:T(8,128)} %bitcast.1, s32[2,2,4,512]{3,2,1,0:T(4,128)} %pn_hbm.1, f32[2,2,4,512]{3,2,1,0:T(4,128)} %pw_hbm.1), custom_call_target="tpu_custom_call" | custom-call | tf_op jit(solution)/shard_map/cg/pallas_call | solution.py:529
  82.9 1.8 %hand_over.1 = (f32[2,128,256]{2,1,0:T(8,128)}, f32[2,128,256]{2,1,0:T(8,128)}) custom-call(f32[2,128,256]{2,1,0:T(8,128)} %get-tuple-element.4.x_in, f32[2,128,256]{2,1,0:T(8,128)} %get-tuple-element.5.r_in), custom_call_target="tpu_custom_call" | custom-call | tf_op jit(solution)/shard_map/hand_over/pallas_call | solution.py:541
